TPU v7x, 512 devices: a whole 4x4x16 slice. The times are simulated.
512 devices in a mesh: ctx: 64 (over z_hi, x, y, core), tp: 8 (over z_lo).
Axes of the slice: x: 4, y: 4, z: 16 (z_hi: 2, z_lo: 8; z = z_hi * 8 + z_lo), core: 2. Of those that a mesh axis runs over, the one named last changes fastest.
Arguments:
- queries: bfloat16 [8192, 8192], P('ctx', 'tp'), may hold values from -8 to 8
- keys: bfloat16 [8192, 1024], P('ctx', 'tp'), may hold values from -8 to 8
- values: bfloat16 [8192, 1024], P('ctx', 'tp'), may hold values from -6 to 6
- out_weight: bfloat16 [4096, 8192], P('ctx', 'tp'), may hold values from -0.29882812 to 0.29882812
Outputs:
- mixed_out: bfloat16 [8192, 4096], P('ctx', 'tp')
All inputs are finite; a program needn't handle non-finite values.
Results may differ from a plain program's by a relative error of at most 0.012.
Values may be sent and summed in bfloat16 or wider, within the bound.
A program may use at most 128 MiB of HBM per device.

v0:
```python
import math

import jax
import jax.numpy as jnp
from jax import lax
from jax.sharding import PartitionSpec as P

H = 64
KVH = 8
HD = 128


def shifted(value, axis, by):
    count = lax.axis_size(axis)
    return lax.ppermute(value, axis, [(i, (i + by) % count) for i in range(count)])


def body(queries, keys, values, out_weight):
    length = queries.shape[0]
    query_width = queries.shape[1]
    cycle_size = lax.axis_size("ctx")
    my_index = lax.axis_index("ctx")
    groups = keys.shape[1] // HD
    repeat = H // KVH
    score_scale = 1.0 / math.sqrt(HD)
    kv_pairs = jnp.concatenate([keys, values], axis=1)
    rows_each = length // cycle_size
    moved_queries, moved_pairs = (
        lax.all_to_all(
            queries.reshape(rows_each, cycle_size, query_width),
            "ctx",
            split_axis=1,
            concat_axis=0,
            tiled=True,
        ),
        lax.all_to_all(
            kv_pairs.reshape(rows_each, cycle_size, kv_pairs.shape[1]),
            "ctx",
            split_axis=1,
            concat_axis=0,
            tiled=True,
        ),
    )
    local_queries = moved_queries.reshape(length, query_width)
    local_pairs = moved_pairs.reshape(length, kv_pairs.shape[1])

    def positions(source):
        return source + cycle_size * jnp.arange(length, dtype=jnp.int32)

    query_places = positions(my_index)
    last_query = jnp.max(query_places)
    grouped_queries = local_queries.reshape(length, groups, repeat, HD)

    def update(state, key_block, key_places):
        running_max, denominator, weighted = state
        key_rows = key_block.shape[0]
        key_heads = key_block[:, : groups * HD].reshape(key_rows, groups, HD)
        value_heads = key_block[:, groups * HD :].reshape(key_rows, groups, HD).astype(jnp.float32)
        scores = (
            jnp.einsum(
                "sgrd,kgd->sgrk", grouped_queries, key_heads, preferred_element_type=jnp.float32
            )
            * score_scale
        )
        allowed = key_places[None, :] <= query_places[:, None]
        scores = jnp.where(allowed[:, None, None, :], scores, -1e30)
        new_max = jnp.maximum(running_max, jnp.max(scores, axis=-1))
        rescale = jnp.exp(running_max - new_max)
        weights = jnp.exp(scores - new_max[..., None])
        denominator = denominator * rescale + jnp.sum(weights, axis=-1)
        weighted = weighted * rescale[..., None] + jnp.einsum(
            "sgrk,kgd->sgrd", weights, value_heads
        )
        return (new_max, denominator, weighted)

    def attend(state, key_block, key_places, enabled):
        needed = jnp.logical_and(enabled, jnp.min(key_places) <= last_query)
        return lax.cond(
            needed, lambda held: update(held, key_block, key_places), lambda held: held, state
        )

    initial = (
        jnp.full((length, groups, repeat), -1e30, jnp.float32),
        jnp.zeros((length, groups, repeat), jnp.float32),
        jnp.zeros((length, groups, repeat, HD), jnp.float32),
    )
    state = attend(initial, local_pairs, positions(my_index), jnp.asarray(True))

    def turn_one(turn_index, carried):
        passing_pairs, held = carried
        passing_pairs = shifted(passing_pairs, "ctx", 1)
        held = attend(
            held, passing_pairs, positions((my_index - turn_index) % cycle_size), jnp.asarray(True)
        )
        return (passing_pairs, held)

    state = lax.fori_loop(1, cycle_size, turn_one, (local_pairs, state))[1]
    running_max, denominator, weighted = state
    attended = (weighted / denominator[..., None]).reshape(length, query_width).astype(jnp.bfloat16)
    attended = lax.all_to_all(
        attended.reshape(cycle_size, rows_each, 1, query_width),
        "ctx",
        split_axis=0,
        concat_axis=2,
        tiled=True,
    ).reshape(length, query_width)
    partial_sums = lax.dot_general(
        attended,
        lax.all_gather(out_weight, "ctx", axis=0, tiled=True),
        (((1,), (1,)), ((), ())),
        preferred_element_type=jnp.float32,
    )
    mixed_out = lax.psum_scatter(partial_sums, "tp", scatter_dimension=1, tiled=True)
    return mixed_out.astype(jnp.bfloat16)


def solution(mesh):
    return jax.shard_map(
        body,
        mesh=mesh,
        in_specs=(P("ctx", "tp"), P("ctx", "tp"), P("ctx", "tp"), P("ctx", "tp")),
        out_specs=P("ctx", "tp"),
        check_vma=False,
    )
```

profile of v0, /device:TPU:6, one launch (start us, length us, event | category | flops | bytes accessed | tf_op | source)
XLA Modules:
  0.0 1428.6 jit_solution(13064926541282291705)
XLA Ops:
  8.7 21.3 %all-to-all-start = ((bf16[2,64,256]{2,0,1:T(2,128)(2,1)}), bf16[2,64,256]{2,0,1:T(2,128)(2,1)S(1)}, u32[]{:S(2)}, u32[]{:S(2)}) async-start(bf16[2,64,256]{2,0,1:T(2,128)(2,1)} %copy.18), calls=%async_computation | async-start | bytes 131072 | tf_op jit(solution)/shard_map/all_to_all | solution.py:36
  70.2 1136.3 %while.23 = (s32[]{:T(128)}, bf16[128,256]{1,0:T(8,128)(2,1)S(1)}, f32[128,1,8]{0,2,1:T(8,128)S(1)}, f32[128,1,8]{0,2,1:T(8,128)S(1)}, f32[128,1,8,128]{3,0,2,1:...) while((s32[]{:T(128)}, bf16[128,256]{1,0:T(8,128)(2,1)S(1)}, ...), condition=%wide.region_12.13_spmd.clone.clone, body=%wide.region_6.12_spmd.clone.clone.sunk | while | flops 68177680 | bytes 3444140 | solution.py:97
  160.4 27.6 %collective-permute-start = (bf16[128,256]{1,0:T(8,128)(2,1)S(1)}, bf16[128,256]{1,0:T(8,128)(2,1)S(1)}, u32[]{:S(2)}, u32[]{:S(2)}) collective-permute-start(bf16[128,256]{1,0:T(8,128)(2,1)S(1)} %get-tuple-element.474), channel_id=1, source_target_pairs={{0,8},{8,16},{16,24},{24,32},{32,40},{40,48},{48,56},{56,64},{64,7... | collective-permute-start | bytes 196616 | tf_op jit(solution)/shard_map/while/body/eval_jaxpr/ppermute | solution.py:15
  190.8 19.1 %collective-permute-start = (bf16[128,256]{1,0:T(8,128)(2,1)S(1)}, bf16[128,256]{1,0:T(8,128)(2,1)S(1)}, u32[]{:S(2)}, u32[]{:S(2)}) collective-permute-start(bf16[128,256]{1,0:T(8,128)(2,1)S(1)} %get-tuple-element.474), channel_id=1, source_target_pairs={{0,8},{8,16},{16,24},{24,32},{32,40},{40,48},{48,56},{56,64},{64,7... | collective-permute-start | bytes 196616 | tf_op jit(solution)/shard_map/while/body/eval_jaxpr/ppermute | solution.py:15
  212.7 17.5 %collective-permute-start = (bf16[128,256]{1,0:T(8,128)(2,1)S(1)}, bf16[128,256]{1,0:T(8,128)(2,1)S(1)}, u32[]{:S(2)}, u32[]{:S(2)}) collective-permute-start(bf16[128,256]{1,0:T(8,128)(2,1)S(1)} %get-tuple-element.474), channel_id=1, source_target_pairs={{0,8},{8,16},{16,24},{24,32},{32,40},{40,48},{48,56},{56,64},{64,7... | collective-permute-start | bytes 196616 | tf_op jit(solution)/shard_map/while/body/eval_jaxpr/ppermute | solution.py:15
  233.0 16.7 %collective-permute-start = (bf16[128,256]{1,0:T(8,128)(2,1)S(1)}, bf16[128,256]{1,0:T(8,128)(2,1)S(1)}, u32[]{:S(2)}, u32[]{:S(2)}) collective-permute-start(bf16[128,256]{1,0:T(8,128)(2,1)S(1)} %get-tuple-element.474), channel_id=1, source_target_pairs={{0,8},{8,16},{16,24},{24,32},{32,40},{40,48},{48,56},{56,64},{64,7... | collective-permute-start | bytes 196616 | tf_op jit(solution)/shard_map/while/body/eval_jaxpr/ppermute | solution.py:15
  252.5 16.7 %collective-permute-start = (bf16[128,256]{1,0:T(8,128)(2,1)S(1)}, bf16[128,256]{1,0:T(8,128)(2,1)S(1)}, u32[]{:S(2)}, u32[]{:S(2)}) collective-permute-start(bf16[128,256]{1,0:T(8,128)(2,1)S(1)} %get-tuple-element.474), channel_id=1, source_target_pairs={{0,8},{8,16},{16,24},{24,32},{32,40},{40,48},{48,56},{56,64},{64,7... | collective-permute-start | bytes 196616 | tf_op jit(solution)/shard_map/while/body/eval_jaxpr/ppermute | solution.py:15
  272.0 16.7 %collective-permute-start = (bf16[128,256]{1,0:T(8,128)(2,1)S(1)}, bf16[128,256]{1,0:T(8,128)(2,1)S(1)}, u32[]{:S(2)}, u32[]{:S(2)}) collective-permute-start(bf16[128,256]{1,0:T(8,128)(2,1)S(1)} %get-tuple-element.474), channel_id=1, source_target_pairs={{0,8},{8,16},{16,24},{24,32},{32,40},{40,48},{48,56},{56,64},{64,7... | collective-permute-start | bytes 196616 | tf_op jit(solution)/shard_map/while/body/eval_jaxpr/ppermute | solution.py:15
  291.4 16.7 %collective-permute-start = (bf16[128,256]{1,0:T(8,128)(2,1)S(1)}, bf16[128,256]{1,0:T(8,128)(2,1)S(1)}, u32[]{:S(2)}, u32[]{:S(2)}) collective-permute-start(bf16[128,256]{1,0:T(8,128)(2,1)S(1)} %get-tuple-element.474), channel_id=1, source_target_pairs={{0,8},{8,16},{16,24},{24,32},{32,40},{40,48},{48,56},{56,64},{64,7... | collective-permute-start | bytes 196616 | tf_op jit(solution)/shard_map/while/body/eval_jaxpr/ppermute | solution.py:15
  310.9 16.7 %collective-permute-start = (bf16[128,256]{1,0:T(8,128)(2,1)S(1)}, bf16[128,256]{1,0:T(8,128)(2,1)S(1)}, u32[]{:S(2)}, u32[]{:S(2)}) collective-permute-start(bf16[128,256]{1,0:T(8,128)(2,1)S(1)} %get-tuple-element.474), channel_id=1, source_target_pairs={{0,8},{8,16},{16,24},{24,32},{32,40},{40,48},{48,56},{56,64},{64,7... | collective-permute-start | bytes 196616 | tf_op jit(solution)/shard_map/while/body/eval_jaxpr/ppermute | solution.py:15
  330.4 16.7 %collective-permute-start = (bf16[128,256]{1,0:T(8,128)(2,1)S(1)}, bf16[128,256]{1,0:T(8,128)(2,1)S(1)}, u32[]{:S(2)}, u32[]{:S(2)}) collective-permute-start(bf16[128,256]{1,0:T(8,128)(2,1)S(1)} %get-tuple-element.474), channel_id=1, source_target_pairs={{0,8},{8,16},{16,24},{24,32},{32,40},{40,48},{48,56},{56,64},{64,7... | collective-permute-start | bytes 196616 | tf_op jit(solution)/shard_map/while/body/eval_jaxpr/ppermute | solution.py:15
  349.8 16.7 %collective-permute-start = (bf16[128,256]{1,0:T(8,128)(2,1)S(1)}, bf16[128,256]{1,0:T(8,128)(2,1)S(1)}, u32[]{:S(2)}, u32[]{:S(2)}) collective-permute-start(bf16[128,256]{1,0:T(8,128)(2,1)S(1)} %get-tuple-element.474), channel_id=1, source_target_pairs={{0,8},{8,16},{16,24},{24,32},{32,40},{40,48},{48,56},{56,64},{64,7... | collective-permute-start | bytes 196616 | tf_op jit(solution)/shard_map/while/body/eval_jaxpr/ppermute | solution.py:15
  369.3 16.7 %collective-permute-start = (bf16[128,256]{1,0:T(8,128)(2,1)S(1)}, bf16[128,256]{1,0:T(8,128)(2,1)S(1)}, u32[]{:S(2)}, u32[]{:S(2)}) collective-permute-start(bf16[128,256]{1,0:T(8,128)(2,1)S(1)} %get-tuple-element.474), channel_id=1, source_target_pairs={{0,8},{8,16},{16,24},{24,32},{32,40},{40,48},{48,56},{56,64},{64,7... | collective-permute-start | bytes 196616 | tf_op jit(solution)/shard_map/while/body/eval_jaxpr/ppermute | solution.py:15
  388.8 16.7 %collective-permute-start = (bf16[128,256]{1,0:T(8,128)(2,1)S(1)}, bf16[128,256]{1,0:T(8,128)(2,1)S(1)}, u32[]{:S(2)}, u32[]{:S(2)}) collective-permute-start(bf16[128,256]{1,0:T(8,128)(2,1)S(1)} %get-tuple-element.474), channel_id=1, source_target_pairs={{0,8},{8,16},{16,24},{24,32},{32,40},{40,48},{48,56},{56,64},{64,7... | collective-permute-start | bytes 196616 | tf_op jit(solution)/shard_map/while/body/eval_jaxpr/ppermute | solution.py:15
  408.3 16.7 %collective-permute-start = (bf16[128,256]{1,0:T(8,128)(2,1)S(1)}, bf16[128,256]{1,0:T(8,128)(2,1)S(1)}, u32[]{:S(2)}, u32[]{:S(2)}) collective-permute-start(bf16[128,256]{1,0:T(8,128)(2,1)S(1)} %get-tuple-element.474), channel_id=1, source_target_pairs={{0,8},{8,16},{16,24},{24,32},{32,40},{40,48},{48,56},{56,64},{64,7... | collective-permute-start | bytes 196616 | tf_op jit(solution)/shard_map/while/body/eval_jaxpr/ppermute | solution.py:15
  427.7 16.7 %collective-permute-start = (bf16[128,256]{1,0:T(8,128)(2,1)S(1)}, bf16[128,256]{1,0:T(8,128)(2,1)S(1)}, u32[]{:S(2)}, u32[]{:S(2)}) collective-permute-start(bf16[128,256]{1,0:T(8,128)(2,1)S(1)} %get-tuple-element.474), channel_id=1, source_target_pairs={{0,8},{8,16},{16,24},{24,32},{32,40},{40,48},{48,56},{56,64},{64,7... | collective-permute-start | bytes 196616 | tf_op jit(solution)/shard_map/while/body/eval_jaxpr/ppermute | solution.py:15
  447.2 16.7 %collective-permute-start = (bf16[128,256]{1,0:T(8,128)(2,1)S(1)}, bf16[128,256]{1,0:T(8,128)(2,1)S(1)}, u32[]{:S(2)}, u32[]{:S(2)}) collective-permute-start(bf16[128,256]{1,0:T(8,128)(2,1)S(1)} %get-tuple-element.474), channel_id=1, source_target_pairs={{0,8},{8,16},{16,24},{24,32},{32,40},{40,48},{48,56},{56,64},{64,7... | collective-permute-start | bytes 196616 | tf_op jit(solution)/shard_map/while/body/eval_jaxpr/ppermute | solution.py:15
  466.7 16.7 %collective-permute-start = (bf16[128,256]{1,0:T(8,128)(2,1)S(1)}, bf16[128,256]{1,0:T(8,128)(2,1)S(1)}, u32[]{:S(2)}, u32[]{:S(2)}) collective-permute-start(bf16[128,256]{1,0:T(8,128)(2,1)S(1)} %get-tuple-element.474), channel_id=1, source_target_pairs={{0,8},{8,16},{16,24},{24,32},{32,40},{40,48},{48,56},{56,64},{64,7... | collective-permute-start | bytes 196616 | tf_op jit(solution)/shard_map/while/body/eval_jaxpr/ppermute | solution.py:15
  486.1 16.7 %collective-permute-start = (bf16[128,256]{1,0:T(8,128)(2,1)S(1)}, bf16[128,256]{1,0:T(8,128)(2,1)S(1)}, u32[]{:S(2)}, u32[]{:S(2)}) collective-permute-start(bf16[128,256]{1,0:T(8,128)(2,1)S(1)} %get-tuple-element.474), channel_id=1, source_target_pairs={{0,8},{8,16},{16,24},{24,32},{32,40},{40,48},{48,56},{56,64},{64,7... | collective-permute-start | bytes 196616 | tf_op jit(solution)/shard_map/while/body/eval_jaxpr/ppermute | solution.py:15
  505.6 16.7 %collective-permute-start = (bf16[128,256]{1,0:T(8,128)(2,1)S(1)}, bf16[128,256]{1,0:T(8,128)(2,1)S(1)}, u32[]{:S(2)}, u32[]{:S(2)}) collective-permute-start(bf16[128,256]{1,0:T(8,128)(2,1)S(1)} %get-tuple-element.474), channel_id=1, source_target_pairs={{0,8},{8,16},{16,24},{24,32},{32,40},{40,48},{48,56},{56,64},{64,7... | collective-permute-start | bytes 196616 | tf_op jit(solution)/shard_map/while/body/eval_jaxpr/ppermute | solution.py:15
  525.1 16.7 %collective-permute-start = (bf16[128,256]{1,0:T(8,128)(2,1)S(1)}, bf16[128,256]{1,0:T(8,128)(2,1)S(1)}, u32[]{:S(2)}, u32[]{:S(2)}) collective-permute-start(bf16[128,256]{1,0:T(8,128)(2,1)S(1)} %get-tuple-element.474), channel_id=1, source_target_pairs={{0,8},{8,16},{16,24},{24,32},{32,40},{40,48},{48,56},{56,64},{64,7... | collective-permute-start | bytes 196616 | tf_op jit(solution)/shard_map/while/body/eval_jaxpr/ppermute | solution.py:15
  544.5 16.7 %collective-permute-start = (bf16[128,256]{1,0:T(8,128)(2,1)S(1)}, bf16[128,256]{1,0:T(8,128)(2,1)S(1)}, u32[]{:S(2)}, u32[]{:S(2)}) collective-permute-start(bf16[128,256]{1,0:T(8,128)(2,1)S(1)} %get-tuple-element.474), channel_id=1, source_target_pairs={{0,8},{8,16},{16,24},{24,32},{32,40},{40,48},{48,56},{56,64},{64,7... | collective-permute-start | bytes 196616 | tf_op jit(solution)/shard_map/while/body/eval_jaxpr/ppermute | solution.py:15
  564.0 16.7 %collective-permute-start = (bf16[128,256]{1,0:T(8,128)(2,1)S(1)}, bf16[128,256]{1,0:T(8,128)(2,1)S(1)}, u32[]{:S(2)}, u32[]{:S(2)}) collective-permute-start(bf16[128,256]{1,0:T(8,128)(2,1)S(1)} %get-tuple-element.474), channel_id=1, source_target_pairs={{0,8},{8,16},{16,24},{24,32},{32,40},{40,48},{48,56},{56,64},{64,7... | collective-permute-start | bytes 196616 | tf_op jit(solution)/shard_map/while/body/eval_jaxpr/ppermute | solution.py:15
  583.5 16.7 %collective-permute-start = (bf16[128,256]{1,0:T(8,128)(2,1)S(1)}, bf16[128,256]{1,0:T(8,128)(2,1)S(1)}, u32[]{:S(2)}, u32[]{:S(2)}) collective-permute-start(bf16[128,256]{1,0:T(8,128)(2,1)S(1)} %get-tuple-element.474), channel_id=1, source_target_pairs={{0,8},{8,16},{16,24},{24,32},{32,40},{40,48},{48,56},{56,64},{64,7... | collective-permute-start | bytes 196616 | tf_op jit(solution)/shard_map/while/body/eval_jaxpr/ppermute | solution.py:15
  603.0 16.7 %collective-permute-start = (bf16[128,256]{1,0:T(8,128)(2,1)S(1)}, bf16[128,256]{1,0:T(8,128)(2,1)S(1)}, u32[]{:S(2)}, u32[]{:S(2)}) collective-permute-start(bf16[128,256]{1,0:T(8,128)(2,1)S(1)} %get-tuple-element.474), channel_id=1, source_target_pairs={{0,8},{8,16},{16,24},{24,32},{32,40},{40,48},{48,56},{56,64},{64,7... | collective-permute-start | bytes 196616 | tf_op jit(solution)/shard_map/while/body/eval_jaxpr/ppermute | solution.py:15
  622.4 16.7 %collective-permute-start = (bf16[128,256]{1,0:T(8,128)(2,1)S(1)}, bf16[128,256]{1,0:T(8,128)(2,1)S(1)}, u32[]{:S(2)}, u32[]{:S(2)}) collective-permute-start(bf16[128,256]{1,0:T(8,128)(2,1)S(1)} %get-tuple-element.474), channel_id=1, source_target_pairs={{0,8},{8,16},{16,24},{24,32},{32,40},{40,48},{48,56},{56,64},{64,7... | collective-permute-start | bytes 196616 | tf_op jit(solution)/shard_map/while/body/eval_jaxpr/ppermute | solution.py:15
  641.9 16.7 %collective-permute-start = (bf16[128,256]{1,0:T(8,128)(2,1)S(1)}, bf16[128,256]{1,0:T(8,128)(2,1)S(1)}, u32[]{:S(2)}, u32[]{:S(2)}) collective-permute-start(bf16[128,256]{1,0:T(8,128)(2,1)S(1)} %get-tuple-element.474), channel_id=1, source_target_pairs={{0,8},{8,16},{16,24},{24,32},{32,40},{40,48},{48,56},{56,64},{64,7... | collective-permute-start | bytes 196616 | tf_op jit(solution)/shard_map/while/body/eval_jaxpr/ppermute | solution.py:15
  661.4 16.7 %collective-permute-start = (bf16[128,256]{1,0:T(8,128)(2,1)S(1)}, bf16[128,256]{1,0:T(8,128)(2,1)S(1)}, u32[]{:S(2)}, u32[]{:S(2)}) collective-permute-start(bf16[128,256]{1,0:T(8,128)(2,1)S(1)} %get-tuple-element.474), channel_id=1, source_target_pairs={{0,8},{8,16},{16,24},{24,32},{32,40},{40,48},{48,56},{56,64},{64,7... | collective-permute-start | bytes 196616 | tf_op jit(solution)/shard_map/while/body/eval_jaxpr/ppermute | solution.py:15
  680.8 16.7 %collective-permute-start = (bf16[128,256]{1,0:T(8,128)(2,1)S(1)}, bf16[128,256]{1,0:T(8,128)(2,1)S(1)}, u32[]{:S(2)}, u32[]{:S(2)}) collective-permute-start(bf16[128,256]{1,0:T(8,128)(2,1)S(1)} %get-tuple-element.474), channel_id=1, source_target_pairs={{0,8},{8,16},{16,24},{24,32},{32,40},{40,48},{48,56},{56,64},{64,7... | collective-permute-start | bytes 196616 | tf_op jit(solution)/shard_map/while/body/eval_jaxpr/ppermute | solution.py:15
  700.3 16.7 %collective-permute-start = (bf16[128,256]{1,0:T(8,128)(2,1)S(1)}, bf16[128,256]{1,0:T(8,128)(2,1)S(1)}, u32[]{:S(2)}, u32[]{:S(2)}) collective-permute-start(bf16[128,256]{1,0:T(8,128)(2,1)S(1)} %get-tuple-element.474), channel_id=1, source_target_pairs={{0,8},{8,16},{16,24},{24,32},{32,40},{40,48},{48,56},{56,64},{64,7... | collective-permute-start | bytes 196616 | tf_op jit(solution)/shard_map/while/body/eval_jaxpr/ppermute | solution.py:15
  719.8 16.7 %collective-permute-start = (bf16[128,256]{1,0:T(8,128)(2,1)S(1)}, bf16[128,256]{1,0:T(8,128)(2,1)S(1)}, u32[]{:S(2)}, u32[]{:S(2)}) collective-permute-start(bf16[128,256]{1,0:T(8,128)(2,1)S(1)} %get-tuple-element.474), channel_id=1, source_target_pairs={{0,8},{8,16},{16,24},{24,32},{32,40},{40,48},{48,56},{56,64},{64,7... | collective-permute-start | bytes 196616 | tf_op jit(solution)/shard_map/while/body/eval_jaxpr/ppermute | solution.py:15
  739.2 16.7 %collective-permute-start = (bf16[128,256]{1,0:T(8,128)(2,1)S(1)}, bf16[128,256]{1,0:T(8,128)(2,1)S(1)}, u32[]{:S(2)}, u32[]{:S(2)}) collective-permute-start(bf16[128,256]{1,0:T(8,128)(2,1)S(1)} %get-tuple-element.474), channel_id=1, source_target_pairs={{0,8},{8,16},{16,24},{24,32},{32,40},{40,48},{48,56},{56,64},{64,7... | collective-permute-start | bytes 196616 | tf_op jit(solution)/shard_map/while/body/eval_jaxpr/ppermute | solution.py:15
  758.7 16.7 %collective-permute-start = (bf16[128,256]{1,0:T(8,128)(2,1)S(1)}, bf16[128,256]{1,0:T(8,128)(2,1)S(1)}, u32[]{:S(2)}, u32[]{:S(2)}) collective-permute-start(bf16[128,256]{1,0:T(8,128)(2,1)S(1)} %get-tuple-element.474), channel_id=1, source_target_pairs={{0,8},{8,16},{16,24},{24,32},{32,40},{40,48},{48,56},{56,64},{64,7... | collective-permute-start | bytes 196616 | tf_op jit(solution)/shard_map/while/body/eval_jaxpr/ppermute | solution.py:15
  778.2 16.7 %collective-permute-start = (bf16[128,256]{1,0:T(8,128)(2,1)S(1)}, bf16[128,256]{1,0:T(8,128)(2,1)S(1)}, u32[]{:S(2)}, u32[]{:S(2)}) collective-permute-start(bf16[128,256]{1,0:T(8,128)(2,1)S(1)} %get-tuple-element.474), channel_id=1, source_target_pairs={{0,8},{8,16},{16,24},{24,32},{32,40},{40,48},{48,56},{56,64},{64,7... | collective-permute-start | bytes 196616 | tf_op jit(solution)/shard_map/while/body/eval_jaxpr/ppermute | solution.py:15
  797.6 16.7 %collective-permute-start = (bf16[128,256]{1,0:T(8,128)(2,1)S(1)}, bf16[128,256]{1,0:T(8,128)(2,1)S(1)}, u32[]{:S(2)}, u32[]{:S(2)}) collective-permute-start(bf16[128,256]{1,0:T(8,128)(2,1)S(1)} %get-tuple-element.474), channel_id=1, source_target_pairs={{0,8},{8,16},{16,24},{24,32},{32,40},{40,48},{48,56},{56,64},{64,7... | collective-permute-start | bytes 196616 | tf_op jit(solution)/shard_map/while/body/eval_jaxpr/ppermute | solution.py:15
  817.1 16.7 %collective-permute-start = (bf16[128,256]{1,0:T(8,128)(2,1)S(1)}, bf16[128,256]{1,0:T(8,128)(2,1)S(1)}, u32[]{:S(2)}, u32[]{:S(2)}) collective-permute-start(bf16[128,256]{1,0:T(8,128)(2,1)S(1)} %get-tuple-element.474), channel_id=1, source_target_pairs={{0,8},{8,16},{16,24},{24,32},{32,40},{40,48},{48,56},{56,64},{64,7... | collective-permute-start | bytes 196616 | tf_op jit(solution)/shard_map/while/body/eval_jaxpr/ppermute | solution.py:15
  836.6 16.7 %collective-permute-start = (bf16[128,256]{1,0:T(8,128)(2,1)S(1)}, bf16[128,256]{1,0:T(8,128)(2,1)S(1)}, u32[]{:S(2)}, u32[]{:S(2)}) collective-permute-start(bf16[128,256]{1,0:T(8,128)(2,1)S(1)} %get-tuple-element.474), channel_id=1, source_target_pairs={{0,8},{8,16},{16,24},{24,32},{32,40},{40,48},{48,56},{56,64},{64,7... | collective-permute-start | bytes 196616 | tf_op jit(solution)/shard_map/while/body/eval_jaxpr/ppermute | solution.py:15
  856.1 16.7 %collective-permute-start = (bf16[128,256]{1,0:T(8,128)(2,1)S(1)}, bf16[128,256]{1,0:T(8,128)(2,1)S(1)}, u32[]{:S(2)}, u32[]{:S(2)}) collective-permute-start(bf16[128,256]{1,0:T(8,128)(2,1)S(1)} %get-tuple-element.474), channel_id=1, source_target_pairs={{0,8},{8,16},{16,24},{24,32},{32,40},{40,48},{48,56},{56,64},{64,7... | collective-permute-start | bytes 196616 | tf_op jit(solution)/shard_map/while/body/eval_jaxpr/ppermute | solution.py:15
  875.5 16.7 %collective-permute-start = (bf16[128,256]{1,0:T(8,128)(2,1)S(1)}, bf16[128,256]{1,0:T(8,128)(2,1)S(1)}, u32[]{:S(2)}, u32[]{:S(2)}) collective-permute-start(bf16[128,256]{1,0:T(8,128)(2,1)S(1)} %get-tuple-element.474), channel_id=1, source_target_pairs={{0,8},{8,16},{16,24},{24,32},{32,40},{40,48},{48,56},{56,64},{64,7... | collective-permute-start | bytes 196616 | tf_op jit(solution)/shard_map/while/body/eval_jaxpr/ppermute | solution.py:15
  895.0 16.7 %collective-permute-start = (bf16[128,256]{1,0:T(8,128)(2,1)S(1)}, bf16[128,256]{1,0:T(8,128)(2,1)S(1)}, u32[]{:S(2)}, u32[]{:S(2)}) collective-permute-start(bf16[128,256]{1,0:T(8,128)(2,1)S(1)} %get-tuple-element.474), channel_id=1, source_target_pairs={{0,8},{8,16},{16,24},{24,32},{32,40},{40,48},{48,56},{56,64},{64,7... | collective-permute-start | bytes 196616 | tf_op jit(solution)/shard_map/while/body/eval_jaxpr/ppermute | solution.py:15
  914.5 16.7 %collective-permute-start = (bf16[128,256]{1,0:T(8,128)(2,1)S(1)}, bf16[128,256]{1,0:T(8,128)(2,1)S(1)}, u32[]{:S(2)}, u32[]{:S(2)}) collective-permute-start(bf16[128,256]{1,0:T(8,128)(2,1)S(1)} %get-tuple-element.474), channel_id=1, source_target_pairs={{0,8},{8,16},{16,24},{24,32},{32,40},{40,48},{48,56},{56,64},{64,7... | collective-permute-start | bytes 196616 | tf_op jit(solution)/shard_map/while/body/eval_jaxpr/ppermute | solution.py:15
  933.9 16.7 %collective-permute-start = (bf16[128,256]{1,0:T(8,128)(2,1)S(1)}, bf16[128,256]{1,0:T(8,128)(2,1)S(1)}, u32[]{:S(2)}, u32[]{:S(2)}) collective-permute-start(bf16[128,256]{1,0:T(8,128)(2,1)S(1)} %get-tuple-element.474), channel_id=1, source_target_pairs={{0,8},{8,16},{16,24},{24,32},{32,40},{40,48},{48,56},{56,64},{64,7... | collective-permute-start | bytes 196616 | tf_op jit(solution)/shard_map/while/body/eval_jaxpr/ppermute | solution.py:15
  1011.8 16.7 %collective-permute-start = (bf16[128,256]{1,0:T(8,128)(2,1)S(1)}, bf16[128,256]{1,0:T(8,128)(2,1)S(1)}, u32[]{:S(2)}, u32[]{:S(2)}) collective-permute-start(bf16[128,256]{1,0:T(8,128)(2,1)S(1)} %get-tuple-element.474), channel_id=1, source_target_pairs={{0,8},{8,16},{16,24},{24,32},{32,40},{40,48},{48,56},{56,64},{64,7... | collective-permute-start | bytes 196616 | tf_op jit(solution)/shard_map/while/body/eval_jaxpr/ppermute | solution.py:15
  1070.2 16.7 %collective-permute-start = (bf16[128,256]{1,0:T(8,128)(2,1)S(1)}, bf16[128,256]{1,0:T(8,128)(2,1)S(1)}, u32[]{:S(2)}, u32[]{:S(2)}) collective-permute-start(bf16[128,256]{1,0:T(8,128)(2,1)S(1)} %get-tuple-element.474), channel_id=1, source_target_pairs={{0,8},{8,16},{16,24},{24,32},{32,40},{40,48},{48,56},{56,64},{64,7... | collective-permute-start | bytes 196616 | tf_op jit(solution)/shard_map/while/body/eval_jaxpr/ppermute | solution.py:15
  1128.6 16.7 %collective-permute-start = (bf16[128,256]{1,0:T(8,128)(2,1)S(1)}, bf16[128,256]{1,0:T(8,128)(2,1)S(1)}, u32[]{:S(2)}, u32[]{:S(2)}) collective-permute-start(bf16[128,256]{1,0:T(8,128)(2,1)S(1)} %get-tuple-element.474), channel_id=1, source_target_pairs={{0,8},{8,16},{16,24},{24,32},{32,40},{40,48},{48,56},{56,64},{64,7... | collective-permute-start | bytes 196616 | tf_op jit(solution)/shard_map/while/body/eval_jaxpr/ppermute | solution.py:15
  1187.0 16.7 %collective-permute-start = (bf16[128,256]{1,0:T(8,128)(2,1)S(1)}, bf16[128,256]{1,0:T(8,128)(2,1)S(1)}, u32[]{:S(2)}, u32[]{:S(2)}) collective-permute-start(bf16[128,256]{1,0:T(8,128)(2,1)S(1)} %get-tuple-element.474), channel_id=1, source_target_pairs={{0,8},{8,16},{16,24},{24,32},{32,40},{40,48},{48,56},{56,64},{64,7... | collective-permute-start | bytes 196616 | tf_op jit(solution)/shard_map/while/body/eval_jaxpr/ppermute | solution.py:15
  1207.0 134.2 %all_to_all.45 = bf16[64,2,1,1024]{3,1,2,0:T(2,128)(2,1)S(1)} all-to-all(bf16[64,2,1,1024]{3,1,2,0:T(2,128)(2,1)S(1)} %bitcast.103), channel_id=1, replica_groups=mesh['ctx'=64,'tp'=8] {'ctx'}, dimensions={0} | all-to-all | bytes 524288 | tf_op jit(solution)/shard_map/all_to_all | solution.py:100
  1348.9 71.2 %reduce-scatter.2.cloned.1.call-done = f32[128,512]{1,0:T(8,128)} async-done(((f32[128,4096]{1,0:T(8,128)}), f32[128,512]{1,0:T(8,128)}) %reduce-scatter.2.cloned.1.call-update) | async-done | bytes 262160 | tf_op jit(solution)/shard_map/reduce_scatter | solution.py:113
  (868 shorter events, 418.2 us)
Async XLA Ops:
  6.5 1334.7 %all-gather.2.cloned.1.call-start = ((), (), s32[]{:S(2)}) async-start(), calls=%async_computation.4 | async-start | bytes 8519680 | tf_op jit(solution)/shard_map/all_gather | solution.py:109
  8.7 36.6 %all-to-all-start = ((bf16[2,64,256]{2,0,1:T(2,128)(2,1)}), bf16[2,64,256]{2,0,1:T(2,128)(2,1)S(1)}, u32[]{:S(2)}, u32[]{:S(2)}) async-start(bf16[2,64,256]{2,0,1:T(2,128)(2,1)} %copy.18), calls=%async_computation | async-start | bytes 131072 | tf_op jit(solution)/shard_map/all_to_all | solution.py:36
  45.3 23.8 %all-to-all-start.1 = ((bf16[2,64,1024]{2,0,1:T(2,128)(2,1)}), bf16[2,64,1024]{2,0,1:T(2,128)(2,1)S(1)}, u32[]{:S(2)}, u32[]{:S(2)}) async-start(bf16[2,64,1024]{2,0,1:T(2,128)(2,1)} %copy.19), calls=%async_computation.1 | async-start | bytes 524288 | tf_op jit(solution)/shard_map/all_to_all | solution.py:29
  51.5 1368.7 %reduce-scatter.2.cloned.1.call-start = ((), (), s32[]{:S(2)}) async-start(), calls=%async_computation.5 | async-start | bytes 2359296 | tf_op jit(solution)/shard_map/reduce_scatter | solution.py:113
  160.4 29.4 %collective-permute-start = (bf16[128,256]{1,0:T(8,128)(2,1)S(1)}, bf16[128,256]{1,0:T(8,128)(2,1)S(1)}, u32[]{:S(2)}, u32[]{:S(2)}) collective-permute-start(bf16[128,256]{1,0:T(8,128)(2,1)S(1)} %get-tuple-element.474), channel_id=1, source_target_pairs={{0,8},{8,16},{16,24},{24,32},{32,40},{40,48},{48,56},{56,64},{64,7... | collective-permute-start | bytes 196616 | tf_op jit(solution)/shard_map/while/body/eval_jaxpr/ppermute | solution.py:15
  190.8 20.9 %collective-permute-start = (bf16[128,256]{1,0:T(8,128)(2,1)S(1)}, bf16[128,256]{1,0:T(8,128)(2,1)S(1)}, u32[]{:S(2)}, u32[]{:S(2)}) collective-permute-start(bf16[128,256]{1,0:T(8,128)(2,1)S(1)} %get-tuple-element.474), channel_id=1, source_target_pairs={{0,8},{8,16},{16,24},{24,32},{32,40},{40,48},{48,56},{56,64},{64,7... | collective-permute-start | bytes 196616 | tf_op jit(solution)/shard_map/while/body/eval_jaxpr/ppermute | solution.py:15
  212.7 19.3 %collective-permute-start = (bf16[128,256]{1,0:T(8,128)(2,1)S(1)}, bf16[128,256]{1,0:T(8,128)(2,1)S(1)}, u32[]{:S(2)}, u32[]{:S(2)}) collective-permute-start(bf16[128,256]{1,0:T(8,128)(2,1)S(1)} %get-tuple-element.474), channel_id=1, source_target_pairs={{0,8},{8,16},{16,24},{24,32},{32,40},{40,48},{48,56},{56,64},{64,7... | collective-permute-start | bytes 196616 | tf_op jit(solution)/shard_map/while/body/eval_jaxpr/ppermute | solution.py:15
  233.0 18.5 %collective-permute-start = (bf16[128,256]{1,0:T(8,128)(2,1)S(1)}, bf16[128,256]{1,0:T(8,128)(2,1)S(1)}, u32[]{:S(2)}, u32[]{:S(2)}) collective-permute-start(bf16[128,256]{1,0:T(8,128)(2,1)S(1)} %get-tuple-element.474), channel_id=1, source_target_pairs={{0,8},{8,16},{16,24},{24,32},{32,40},{40,48},{48,56},{56,64},{64,7... | collective-permute-start | bytes 196616 | tf_op jit(solution)/shard_map/while/body/eval_jaxpr/ppermute | solution.py:15
  252.5 18.5 %collective-permute-start = (bf16[128,256]{1,0:T(8,128)(2,1)S(1)}, bf16[128,256]{1,0:T(8,128)(2,1)S(1)}, u32[]{:S(2)}, u32[]{:S(2)}) collective-permute-start(bf16[128,256]{1,0:T(8,128)(2,1)S(1)} %get-tuple-element.474), channel_id=1, source_target_pairs={{0,8},{8,16},{16,24},{24,32},{32,40},{40,48},{48,56},{56,64},{64,7... | collective-permute-start | bytes 196616 | tf_op jit(solution)/shard_map/while/body/eval_jaxpr/ppermute | solution.py:15
  272.0 18.5 %collective-permute-start = (bf16[128,256]{1,0:T(8,128)(2,1)S(1)}, bf16[128,256]{1,0:T(8,128)(2,1)S(1)}, u32[]{:S(2)}, u32[]{:S(2)}) collective-permute-start(bf16[128,256]{1,0:T(8,128)(2,1)S(1)} %get-tuple-element.474), channel_id=1, source_target_pairs={{0,8},{8,16},{16,24},{24,32},{32,40},{40,48},{48,56},{56,64},{64,7... | collective-permute-start | bytes 196616 | tf_op jit(solution)/shard_map/while/body/eval_jaxpr/ppermute | solution.py:15
  291.4 18.5 %collective-permute-start = (bf16[128,256]{1,0:T(8,128)(2,1)S(1)}, bf16[128,256]{1,0:T(8,128)(2,1)S(1)}, u32[]{:S(2)}, u32[]{:S(2)}) collective-permute-start(bf16[128,256]{1,0:T(8,128)(2,1)S(1)} %get-tuple-element.474), channel_id=1, source_target_pairs={{0,8},{8,16},{16,24},{24,32},{32,40},{40,48},{48,56},{56,64},{64,7... | collective-permute-start | bytes 196616 | tf_op jit(solution)/shard_map/while/body/eval_jaxpr/ppermute | solution.py:15
  310.9 18.5 %collective-permute-start = (bf16[128,256]{1,0:T(8,128)(2,1)S(1)}, bf16[128,256]{1,0:T(8,128)(2,1)S(1)}, u32[]{:S(2)}, u32[]{:S(2)}) collective-permute-start(bf16[128,256]{1,0:T(8,128)(2,1)S(1)} %get-tuple-element.474), channel_id=1, source_target_pairs={{0,8},{8,16},{16,24},{24,32},{32,40},{40,48},{48,56},{56,64},{64,7... | collective-permute-start | bytes 196616 | tf_op jit(solution)/shard_map/while/body/eval_jaxpr/ppermute | solution.py:15
  330.4 18.5 %collective-permute-start = (bf16[128,256]{1,0:T(8,128)(2,1)S(1)}, bf16[128,256]{1,0:T(8,128)(2,1)S(1)}, u32[]{:S(2)}, u32[]{:S(2)}) collective-permute-start(bf16[128,256]{1,0:T(8,128)(2,1)S(1)} %get-tuple-element.474), channel_id=1, source_target_pairs={{0,8},{8,16},{16,24},{24,32},{32,40},{40,48},{48,56},{56,64},{64,7... | collective-permute-start | bytes 196616 | tf_op jit(solution)/shard_map/while/body/eval_jaxpr/ppermute | solution.py:15
  349.8 18.5 %collective-permute-start = (bf16[128,256]{1,0:T(8,128)(2,1)S(1)}, bf16[128,256]{1,0:T(8,128)(2,1)S(1)}, u32[]{:S(2)}, u32[]{:S(2)}) collective-permute-start(bf16[128,256]{1,0:T(8,128)(2,1)S(1)} %get-tuple-element.474), channel_id=1, source_target_pairs={{0,8},{8,16},{16,24},{24,32},{32,40},{40,48},{48,56},{56,64},{64,7... | collective-permute-start | bytes 196616 | tf_op jit(solution)/shard_map/while/body/eval_jaxpr/ppermute | solution.py:15
  369.3 18.5 %collective-permute-start = (bf16[128,256]{1,0:T(8,128)(2,1)S(1)}, bf16[128,256]{1,0:T(8,128)(2,1)S(1)}, u32[]{:S(2)}, u32[]{:S(2)}) collective-permute-start(bf16[128,256]{1,0:T(8,128)(2,1)S(1)} %get-tuple-element.474), channel_id=1, source_target_pairs={{0,8},{8,16},{16,24},{24,32},{32,40},{40,48},{48,56},{56,64},{64,7... | collective-permute-start | bytes 196616 | tf_op jit(solution)/shard_map/while/body/eval_jaxpr/ppermute | solution.py:15
  388.8 18.5 %collective-permute-start = (bf16[128,256]{1,0:T(8,128)(2,1)S(1)}, bf16[128,256]{1,0:T(8,128)(2,1)S(1)}, u32[]{:S(2)}, u32[]{:S(2)}) collective-permute-start(bf16[128,256]{1,0:T(8,128)(2,1)S(1)} %get-tuple-element.474), channel_id=1, source_target_pairs={{0,8},{8,16},{16,24},{24,32},{32,40},{40,48},{48,56},{56,64},{64,7... | collective-permute-start | bytes 196616 | tf_op jit(solution)/shard_map/while/body/eval_jaxpr/ppermute | solution.py:15
  408.3 18.5 %collective-permute-start = (bf16[128,256]{1,0:T(8,128)(2,1)S(1)}, bf16[128,256]{1,0:T(8,128)(2,1)S(1)}, u32[]{:S(2)}, u32[]{:S(2)}) collective-permute-start(bf16[128,256]{1,0:T(8,128)(2,1)S(1)} %get-tuple-element.474), channel_id=1, source_target_pairs={{0,8},{8,16},{16,24},{24,32},{32,40},{40,48},{48,56},{56,64},{64,7... | collective-permute-start | bytes 196616 | tf_op jit(solution)/shard_map/while/body/eval_jaxpr/ppermute | solution.py:15
  427.7 18.5 %collective-permute-start = (bf16[128,256]{1,0:T(8,128)(2,1)S(1)}, bf16[128,256]{1,0:T(8,128)(2,1)S(1)}, u32[]{:S(2)}, u32[]{:S(2)}) collective-permute-start(bf16[128,256]{1,0:T(8,128)(2,1)S(1)} %get-tuple-element.474), channel_id=1, source_target_pairs={{0,8},{8,16},{16,24},{24,32},{32,40},{40,48},{48,56},{56,64},{64,7... | collective-permute-start | bytes 196616 | tf_op jit(solution)/shard_map/while/body/eval_jaxpr/ppermute | solution.py:15
  447.2 18.5 %collective-permute-start = (bf16[128,256]{1,0:T(8,128)(2,1)S(1)}, bf16[128,256]{1,0:T(8,128)(2,1)S(1)}, u32[]{:S(2)}, u32[]{:S(2)}) collective-permute-start(bf16[128,256]{1,0:T(8,128)(2,1)S(1)} %get-tuple-element.474), channel_id=1, source_target_pairs={{0,8},{8,16},{16,24},{24,32},{32,40},{40,48},{48,56},{56,64},{64,7... | collective-permute-start | bytes 196616 | tf_op jit(solution)/shard_map/while/body/eval_jaxpr/ppermute | solution.py:15
  466.7 18.5 %collective-permute-start = (bf16[128,256]{1,0:T(8,128)(2,1)S(1)}, bf16[128,256]{1,0:T(8,128)(2,1)S(1)}, u32[]{:S(2)}, u32[]{:S(2)}) collective-permute-start(bf16[128,256]{1,0:T(8,128)(2,1)S(1)} %get-tuple-element.474), channel_id=1, source_target_pairs={{0,8},{8,16},{16,24},{24,32},{32,40},{40,48},{48,56},{56,64},{64,7... | collective-permute-start | bytes 196616 | tf_op jit(solution)/shard_map/while/body/eval_jaxpr/ppermute | solution.py:15
  486.1 18.5 %collective-permute-start = (bf16[128,256]{1,0:T(8,128)(2,1)S(1)}, bf16[128,256]{1,0:T(8,128)(2,1)S(1)}, u32[]{:S(2)}, u32[]{:S(2)}) collective-permute-start(bf16[128,256]{1,0:T(8,128)(2,1)S(1)} %get-tuple-element.474), channel_id=1, source_target_pairs={{0,8},{8,16},{16,24},{24,32},{32,40},{40,48},{48,56},{56,64},{64,7... | collective-permute-start | bytes 196616 | tf_op jit(solution)/shard_map/while/body/eval_jaxpr/ppermute | solution.py:15
  525.1 18.5 %collective-permute-start = (bf16[128,256]{1,0:T(8,128)(2,1)S(1)}, bf16[128,256]{1,0:T(8,128)(2,1)S(1)}, u32[]{:S(2)}, u32[]{:S(2)}) collective-permute-start(bf16[128,256]{1,0:T(8,128)(2,1)S(1)} %get-tuple-element.474), channel_id=1, source_target_pairs={{0,8},{8,16},{16,24},{24,32},{32,40},{40,48},{48,56},{56,64},{64,7... | collective-permute-start | bytes 196616 | tf_op jit(solution)/shard_map/while/body/eval_jaxpr/ppermute | solution.py:15
  544.5 18.5 %collective-permute-start = (bf16[128,256]{1,0:T(8,128)(2,1)S(1)}, bf16[128,256]{1,0:T(8,128)(2,1)S(1)}, u32[]{:S(2)}, u32[]{:S(2)}) collective-permute-start(bf16[128,256]{1,0:T(8,128)(2,1)S(1)} %get-tuple-element.474), channel_id=1, source_target_pairs={{0,8},{8,16},{16,24},{24,32},{32,40},{40,48},{48,56},{56,64},{64,7... | collective-permute-start | bytes 196616 | tf_op jit(solution)/shard_map/while/body/eval_jaxpr/ppermute | solution.py:15
  583.5 18.5 %collective-permute-start = (bf16[128,256]{1,0:T(8,128)(2,1)S(1)}, bf16[128,256]{1,0:T(8,128)(2,1)S(1)}, u32[]{:S(2)}, u32[]{:S(2)}) collective-permute-start(bf16[128,256]{1,0:T(8,128)(2,1)S(1)} %get-tuple-element.474), channel_id=1, source_target_pairs={{0,8},{8,16},{16,24},{24,32},{32,40},{40,48},{48,56},{56,64},{64,7... | collective-permute-start | bytes 196616 | tf_op jit(solution)/shard_map/while/body/eval_jaxpr/ppermute | solution.py:15
  603.0 18.5 %collective-permute-start = (bf16[128,256]{1,0:T(8,128)(2,1)S(1)}, bf16[128,256]{1,0:T(8,128)(2,1)S(1)}, u32[]{:S(2)}, u32[]{:S(2)}) collective-permute-start(bf16[128,256]{1,0:T(8,128)(2,1)S(1)} %get-tuple-element.474), channel_id=1, source_target_pairs={{0,8},{8,16},{16,24},{24,32},{32,40},{40,48},{48,56},{56,64},{64,7... | collective-permute-start | bytes 196616 | tf_op jit(solution)/shard_map/while/body/eval_jaxpr/ppermute | solution.py:15
  641.9 18.5 %collective-permute-start = (bf16[128,256]{1,0:T(8,128)(2,1)S(1)}, bf16[128,256]{1,0:T(8,128)(2,1)S(1)}, u32[]{:S(2)}, u32[]{:S(2)}) collective-permute-start(bf16[128,256]{1,0:T(8,128)(2,1)S(1)} %get-tuple-element.474), channel_id=1, source_target_pairs={{0,8},{8,16},{16,24},{24,32},{32,40},{40,48},{48,56},{56,64},{64,7... | collective-permute-start | bytes 196616 | tf_op jit(solution)/shard_map/while/body/eval_jaxpr/ppermute | solution.py:15
  661.4 18.5 %collective-permute-start = (bf16[128,256]{1,0:T(8,128)(2,1)S(1)}, bf16[128,256]{1,0:T(8,128)(2,1)S(1)}, u32[]{:S(2)}, u32[]{:S(2)}) collective-permute-start(bf16[128,256]{1,0:T(8,128)(2,1)S(1)} %get-tuple-element.474), channel_id=1, source_target_pairs={{0,8},{8,16},{16,24},{24,32},{32,40},{40,48},{48,56},{56,64},{64,7... | collective-permute-start | bytes 196616 | tf_op jit(solution)/shard_map/while/body/eval_jaxpr/ppermute | solution.py:15
  680.8 18.5 %collective-permute-start = (bf16[128,256]{1,0:T(8,128)(2,1)S(1)}, bf16[128,256]{1,0:T(8,128)(2,1)S(1)}, u32[]{:S(2)}, u32[]{:S(2)}) collective-permute-start(bf16[128,256]{1,0:T(8,128)(2,1)S(1)} %get-tuple-element.474), channel_id=1, source_target_pairs={{0,8},{8,16},{16,24},{24,32},{32,40},{40,48},{48,56},{56,64},{64,7... | collective-permute-start | bytes 196616 | tf_op jit(solution)/shard_map/while/body/eval_jaxpr/ppermute | solution.py:15
  700.3 18.5 %collective-permute-start = (bf16[128,256]{1,0:T(8,128)(2,1)S(1)}, bf16[128,256]{1,0:T(8,128)(2,1)S(1)}, u32[]{:S(2)}, u32[]{:S(2)}) collective-permute-start(bf16[128,256]{1,0:T(8,128)(2,1)S(1)} %get-tuple-element.474), channel_id=1, source_target_pairs={{0,8},{8,16},{16,24},{24,32},{32,40},{40,48},{48,56},{56,64},{64,7... | collective-permute-start | bytes 196616 | tf_op jit(solution)/shard_map/while/body/eval_jaxpr/ppermute | solution.py:15
  719.8 18.5 %collective-permute-start = (bf16[128,256]{1,0:T(8,128)(2,1)S(1)}, bf16[128,256]{1,0:T(8,128)(2,1)S(1)}, u32[]{:S(2)}, u32[]{:S(2)}) collective-permute-start(bf16[128,256]{1,0:T(8,128)(2,1)S(1)} %get-tuple-element.474), channel_id=1, source_target_pairs={{0,8},{8,16},{16,24},{24,32},{32,40},{40,48},{48,56},{56,64},{64,7... | collective-permute-start | bytes 196616 | tf_op jit(solution)/shard_map/while/body/eval_jaxpr/ppermute | solution.py:15
  739.2 18.5 %collective-permute-start = (bf16[128,256]{1,0:T(8,128)(2,1)S(1)}, bf16[128,256]{1,0:T(8,128)(2,1)S(1)}, u32[]{:S(2)}, u32[]{:S(2)}) collective-permute-start(bf16[128,256]{1,0:T(8,128)(2,1)S(1)} %get-tuple-element.474), channel_id=1, source_target_pairs={{0,8},{8,16},{16,24},{24,32},{32,40},{40,48},{48,56},{56,64},{64,7... | collective-permute-start | bytes 196616 | tf_op jit(solution)/shard_map/while/body/eval_jaxpr/ppermute | solution.py:15
  758.7 18.5 %collective-permute-start = (bf16[128,256]{1,0:T(8,128)(2,1)S(1)}, bf16[128,256]{1,0:T(8,128)(2,1)S(1)}, u32[]{:S(2)}, u32[]{:S(2)}) collective-permute-start(bf16[128,256]{1,0:T(8,128)(2,1)S(1)} %get-tuple-element.474), channel_id=1, source_target_pairs={{0,8},{8,16},{16,24},{24,32},{32,40},{40,48},{48,56},{56,64},{64,7... | collective-permute-start | bytes 196616 | tf_op jit(solution)/shard_map/while/body/eval_jaxpr/ppermute | solution.py:15
  778.2 18.5 %collective-permute-start = (bf16[128,256]{1,0:T(8,128)(2,1)S(1)}, bf16[128,256]{1,0:T(8,128)(2,1)S(1)}, u32[]{:S(2)}, u32[]{:S(2)}) collective-permute-start(bf16[128,256]{1,0:T(8,128)(2,1)S(1)} %get-tuple-element.474), channel_id=1, source_target_pairs={{0,8},{8,16},{16,24},{24,32},{32,40},{40,48},{48,56},{56,64},{64,7... | collective-permute-start | bytes 196616 | tf_op jit(solution)/shard_map/while/body/eval_jaxpr/ppermute | solution.py:15
  797.6 18.5 %collective-permute-start = (bf16[128,256]{1,0:T(8,128)(2,1)S(1)}, bf16[128,256]{1,0:T(8,128)(2,1)S(1)}, u32[]{:S(2)}, u32[]{:S(2)}) collective-permute-start(bf16[128,256]{1,0:T(8,128)(2,1)S(1)} %get-tuple-element.474), channel_id=1, source_target_pairs={{0,8},{8,16},{16,24},{24,32},{32,40},{40,48},{48,56},{56,64},{64,7... | collective-permute-start | bytes 196616 | tf_op jit(solution)/shard_map/while/body/eval_jaxpr/ppermute | solution.py:15
  817.1 18.5 %collective-permute-start = (bf16[128,256]{1,0:T(8,128)(2,1)S(1)}, bf16[128,256]{1,0:T(8,128)(2,1)S(1)}, u32[]{:S(2)}, u32[]{:S(2)}) collective-permute-start(bf16[128,256]{1,0:T(8,128)(2,1)S(1)} %get-tuple-element.474), channel_id=1, source_target_pairs={{0,8},{8,16},{16,24},{24,32},{32,40},{40,48},{48,56},{56,64},{64,7... | collective-permute-start | bytes 196616 | tf_op jit(solution)/shard_map/while/body/eval_jaxpr/ppermute | solution.py:15
  836.6 18.5 %collective-permute-start = (bf16[128,256]{1,0:T(8,128)(2,1)S(1)}, bf16[128,256]{1,0:T(8,128)(2,1)S(1)}, u32[]{:S(2)}, u32[]{:S(2)}) collective-permute-start(bf16[128,256]{1,0:T(8,128)(2,1)S(1)} %get-tuple-element.474), channel_id=1, source_target_pairs={{0,8},{8,16},{16,24},{24,32},{32,40},{40,48},{48,56},{56,64},{64,7... | collective-permute-start | bytes 196616 | tf_op jit(solution)/shard_map/while/body/eval_jaxpr/ppermute | solution.py:15
  856.1 18.5 %collective-permute-start = (bf16[128,256]{1,0:T(8,128)(2,1)S(1)}, bf16[128,256]{1,0:T(8,128)(2,1)S(1)}, u32[]{:S(2)}, u32[]{:S(2)}) collective-permute-start(bf16[128,256]{1,0:T(8,128)(2,1)S(1)} %get-tuple-element.474), channel_id=1, source_target_pairs={{0,8},{8,16},{16,24},{24,32},{32,40},{40,48},{48,56},{56,64},{64,7... | collective-permute-start | bytes 196616 | tf_op jit(solution)/shard_map/while/body/eval_jaxpr/ppermute | solution.py:15
  895.0 18.5 %collective-permute-start = (bf16[128,256]{1,0:T(8,128)(2,1)S(1)}, bf16[128,256]{1,0:T(8,128)(2,1)S(1)}, u32[]{:S(2)}, u32[]{:S(2)}) collective-permute-start(bf16[128,256]{1,0:T(8,128)(2,1)S(1)} %get-tuple-element.474), channel_id=1, source_target_pairs={{0,8},{8,16},{16,24},{24,32},{32,40},{40,48},{48,56},{56,64},{64,7... | collective-permute-start | bytes 196616 | tf_op jit(solution)/shard_map/while/body/eval_jaxpr/ppermute | solution.py:15
  914.5 18.5 %collective-permute-start = (bf16[128,256]{1,0:T(8,128)(2,1)S(1)}, bf16[128,256]{1,0:T(8,128)(2,1)S(1)}, u32[]{:S(2)}, u32[]{:S(2)}) collective-permute-start(bf16[128,256]{1,0:T(8,128)(2,1)S(1)} %get-tuple-element.474), channel_id=1, source_target_pairs={{0,8},{8,16},{16,24},{24,32},{32,40},{40,48},{48,56},{56,64},{64,7... | collective-permute-start | bytes 196616 | tf_op jit(solution)/shard_map/while/body/eval_jaxpr/ppermute | solution.py:15
  953.4 18.5 %collective-permute-start = (bf16[128,256]{1,0:T(8,128)(2,1)S(1)}, bf16[128,256]{1,0:T(8,128)(2,1)S(1)}, u32[]{:S(2)}, u32[]{:S(2)}) collective-permute-start(bf16[128,256]{1,0:T(8,128)(2,1)S(1)} %get-tuple-element.474), channel_id=1, source_target_pairs={{0,8},{8,16},{16,24},{24,32},{32,40},{40,48},{48,56},{56,64},{64,7... | collective-permute-start | bytes 196616 | tf_op jit(solution)/shard_map/while/body/eval_jaxpr/ppermute | solution.py:15
  972.9 18.5 %collective-permute-start = (bf16[128,256]{1,0:T(8,128)(2,1)S(1)}, bf16[128,256]{1,0:T(8,128)(2,1)S(1)}, u32[]{:S(2)}, u32[]{:S(2)}) collective-permute-start(bf16[128,256]{1,0:T(8,128)(2,1)S(1)} %get-tuple-element.474), channel_id=1, source_target_pairs={{0,8},{8,16},{16,24},{24,32},{32,40},{40,48},{48,56},{56,64},{64,7... | collective-permute-start | bytes 196616 | tf_op jit(solution)/shard_map/while/body/eval_jaxpr/ppermute | solution.py:15
  1011.8 18.5 %collective-permute-start = (bf16[128,256]{1,0:T(8,128)(2,1)S(1)}, bf16[128,256]{1,0:T(8,128)(2,1)S(1)}, u32[]{:S(2)}, u32[]{:S(2)}) collective-permute-start(bf16[128,256]{1,0:T(8,128)(2,1)S(1)} %get-tuple-element.474), channel_id=1, source_target_pairs={{0,8},{8,16},{16,24},{24,32},{32,40},{40,48},{48,56},{56,64},{64,7... | collective-permute-start | bytes 196616 | tf_op jit(solution)/shard_map/while/body/eval_jaxpr/ppermute | solution.py:15
  1031.3 18.5 %collective-permute-start = (bf16[128,256]{1,0:T(8,128)(2,1)S(1)}, bf16[128,256]{1,0:T(8,128)(2,1)S(1)}, u32[]{:S(2)}, u32[]{:S(2)}) collective-permute-start(bf16[128,256]{1,0:T(8,128)(2,1)S(1)} %get-tuple-element.474), channel_id=1, source_target_pairs={{0,8},{8,16},{16,24},{24,32},{32,40},{40,48},{48,56},{56,64},{64,7... | collective-permute-start | bytes 196616 | tf_op jit(solution)/shard_map/while/body/eval_jaxpr/ppermute | solution.py:15
  1050.8 18.5 %collective-permute-start = (bf16[128,256]{1,0:T(8,128)(2,1)S(1)}, bf16[128,256]{1,0:T(8,128)(2,1)S(1)}, u32[]{:S(2)}, u32[]{:S(2)}) collective-permute-start(bf16[128,256]{1,0:T(8,128)(2,1)S(1)} %get-tuple-element.474), channel_id=1, source_target_pairs={{0,8},{8,16},{16,24},{24,32},{32,40},{40,48},{48,56},{56,64},{64,7... | collective-permute-start | bytes 196616 | tf_op jit(solution)/shard_map/while/body/eval_jaxpr/ppermute | solution.py:15
  1070.2 18.5 %collective-permute-start = (bf16[128,256]{1,0:T(8,128)(2,1)S(1)}, bf16[128,256]{1,0:T(8,128)(2,1)S(1)}, u32[]{:S(2)}, u32[]{:S(2)}) collective-permute-start(bf16[128,256]{1,0:T(8,128)(2,1)S(1)} %get-tuple-element.474), channel_id=1, source_target_pairs={{0,8},{8,16},{16,24},{24,32},{32,40},{40,48},{48,56},{56,64},{64,7... | collective-permute-start | bytes 196616 | tf_op jit(solution)/shard_map/while/body/eval_jaxpr/ppermute | solution.py:15
  1089.7 18.5 %collective-permute-start = (bf16[128,256]{1,0:T(8,128)(2,1)S(1)}, bf16[128,256]{1,0:T(8,128)(2,1)S(1)}, u32[]{:S(2)}, u32[]{:S(2)}) collective-permute-start(bf16[128,256]{1,0:T(8,128)(2,1)S(1)} %get-tuple-element.474), channel_id=1, source_target_pairs={{0,8},{8,16},{16,24},{24,32},{32,40},{40,48},{48,56},{56,64},{64,7... | collective-permute-start | bytes 196616 | tf_op jit(solution)/shard_map/while/body/eval_jaxpr/ppermute | solution.py:15
  1109.2 18.5 %collective-permute-start = (bf16[128,256]{1,0:T(8,128)(2,1)S(1)}, bf16[128,256]{1,0:T(8,128)(2,1)S(1)}, u32[]{:S(2)}, u32[]{:S(2)}) collective-permute-start(bf16[128,256]{1,0:T(8,128)(2,1)S(1)} %get-tuple-element.474), channel_id=1, source_target_pairs={{0,8},{8,16},{16,24},{24,32},{32,40},{40,48},{48,56},{56,64},{64,7... | collective-permute-start | bytes 196616 | tf_op jit(solution)/shard_map/while/body/eval_jaxpr/ppermute | solution.py:15
  1128.6 18.5 %collective-permute-start = (bf16[128,256]{1,0:T(8,128)(2,1)S(1)}, bf16[128,256]{1,0:T(8,128)(2,1)S(1)}, u32[]{:S(2)}, u32[]{:S(2)}) collective-permute-start(bf16[128,256]{1,0:T(8,128)(2,1)S(1)} %get-tuple-element.474), channel_id=1, source_target_pairs={{0,8},{8,16},{16,24},{24,32},{32,40},{40,48},{48,56},{56,64},{64,7... | collective-permute-start | bytes 196616 | tf_op jit(solution)/shard_map/while/body/eval_jaxpr/ppermute | solution.py:15
  (19 other events, 246.8 us)
Sparse Core Ops, SparseCore 0:
  11.8 173.5 all-gather.1
  1349.1 71.0 reduce-scatter.1
where the time goes:
time: 1430 us
  starting transfers between devices  951 us (67%)
  waiting for transfers between devices  138 us (10%)
  blocking collectives  134 us (9%)
  loops' own time  81 us (6%)
  other arithmetic  54.9 us (4%)
  matrix products  50.8 us (4%)
  between operations  14.7 us (1%)
    ppermute x63, starting transfers between devices, shifted(): lax.ppermute(value, axis, [(i, (i + by) % count) for i in range(count)])  924 us
    all_to_all x1, blocking collectives, body(): lax.all_to_all(attended.reshape(cycle_size, rows_each, 1, query_width), '...  134 us
    another operation x1, loops' own time, body(): state = lax.fori_loop(1, cycle_size, turn_one, (local_pairs, state))[1]  76.4 us
    reduce_scatter x1, waiting for transfers between devices, body(): lax.psum_scatter(partial_sums, 'tp', scatter_dimension=1, tiled=True)  71.2 us
    reduce_min x64, other arithmetic, attend(): needed = jnp.logical_and(enabled, jnp.min(key_places) <= last_query)  38.9 us
    ppermute x63, waiting for transfers between devices, shifted(): lax.ppermute(value, axis, [(i, (i + by) % count) for i in range(count)])  37.2 us
  transfers between devices with their start and end apart: 67, of which 12 were waited for; matrix products, arithmetic and copies ran while one was open for 7% of the time, Pallas kernels for 0%

commit v1 on v0

v1 whole, which is shorter than its diff:
```python
import math

import jax
import jax.numpy as jnp
from jax import lax
from jax.experimental import pallas as pl
from jax.experimental.pallas import tpu as pltpu
from jax.sharding import PartitionSpec as P

HD = 128
F32 = jnp.float32
BF16 = jnp.bfloat16
SCALE = math.log2(math.e) / math.sqrt(HD)
KEYS = 2048


def attention_kernel(q_ref, k_ref, v_ref, o_ref, acc, peak, total):
    rows = q_ref.shape[0]
    heads = q_ref.shape[1] // HD
    me = lax.axis_index("ctx")
    first = me * rows
    for h in range(heads):
        acc[h] = jnp.zeros((rows, HD), F32)
        peak[h] = jnp.full((rows, HD), -1e30, F32)
        total[h] = jnp.zeros((rows, HD), F32)

    def step(block, masked):
        at = pl.ds(pl.multiple_of(block * KEYS, KEYS), KEYS)
        k = k_ref[at, :]
        v = v_ref[at, :]
        v = jnp.concatenate([v, jnp.ones_like(v)], axis=1)
        if masked:
            row = lax.broadcasted_iota(jnp.int32, (rows, KEYS), 0) + first
            col = lax.broadcasted_iota(jnp.int32, (rows, KEYS), 1) + block * KEYS
            allowed = col <= row
        for h in range(heads):
            s = lax.dot_general(
                q_ref[:, h * HD : (h + 1) * HD], k, (((1,), (1,)), ((), ())), preferred_element_type=F32
            )
            if masked:
                s = jnp.where(allowed, s, -1e30)
            old = peak[h]
            new = jnp.maximum(old, jnp.max(s, axis=1, keepdims=True) * SCALE)
            alpha = jnp.exp2(old - new)
            p = jnp.exp2(s * SCALE - new[:, :1])
            pv = jnp.dot(p.astype(BF16), v, preferred_element_type=F32)
            acc[h] = acc[h] * alpha + pv[:, :HD]
            total[h] = total[h] * alpha + pv[:, HD:]
            peak[h] = new

    full = first // KEYS

    @pl.loop(0, full)
    def _(block):
        step(block, False)

    step(full, True)
    for h in range(heads):
        o_ref[:, h * HD : (h + 1) * HD] = (acc[h] / total[h]).astype(BF16)


def body(queries, keys, values, out_weight):
    rows, width = queries.shape
    heads = width // HD
    all_keys = lax.all_gather(keys, "ctx", axis=0, tiled=True)
    all_values = lax.all_gather(values, "ctx", axis=0, tiled=True)
    all_weight = lax.all_gather(out_weight, "ctx", axis=0, tiled=True)
    attended = pl.pallas_call(
        attention_kernel,
        out_shape=jax.ShapeDtypeStruct((rows, width), BF16),
        in_specs=[pl.BlockSpec(memory_space=pltpu.VMEM)] * 3,
        out_specs=pl.BlockSpec(memory_space=pltpu.VMEM),
        scratch_shapes=[pltpu.VMEM((heads, rows, HD), F32)] * 3,
        compiler_params=pltpu.CompilerParams(vmem_limit_bytes=48 * 2**20),
        cost_estimate=pl.CostEstimate(flops=4 * 10**9, bytes_accessed=5 * 2**20, transcendentals=0),
    )(queries, all_keys, all_values)
    partial_sums = lax.dot_general(
        attended, all_weight, (((1,), (1,)), ((), ())), preferred_element_type=F32
    ).astype(BF16)
    mixed_out = lax.psum_scatter(partial_sums, "tp", scatter_dimension=1, tiled=True)
    return mixed_out


def solution(mesh):
    return jax.shard_map(
        body,
        mesh=mesh,
        in_specs=(P("ctx", "tp"), P("ctx", "tp"), P("ctx", "tp"), P("ctx", "tp")),
        out_specs=P("ctx", "tp"),
        check_vma=False,
    )
```

time: 1430 us -> 473 us (0.33)
  the two profiles are of different devices: /device:TPU:6 before, /device:TPU:4 now
where the time goes in v1:
time: 473 us
  waiting for transfers between devices  442 us (93%)
  between operations  13.1 us (3%)
  matrix products  7.32 us (2%)
  Pallas kernels  6.39 us (1%)
    all_gather x1, waiting for transfers between devices, body(): all_weight = lax.all_gather(out_weight, 'ctx', axis=0, tiled=True)  150 us
    all_gather x1, waiting for transfers between devices, body(): all_keys = lax.all_gather(keys, 'ctx', axis=0, tiled=True)  119 us
    all_gather x1, waiting for transfers between devices, body(): all_values = lax.all_gather(values, 'ctx', axis=0, tiled=True)  106 us
    reduce_scatter x1, waiting for transfers between devices, body(): lax.psum_scatter(partial_sums, 'tp', scatter_dimension=1, tiled=True)  64.8 us
  transfers between devices with their start and end apart: 4, of which 4 were waited for; matrix products, arithmetic and copies ran while one was open for 0% of the time, Pallas kernels for 1%

profile of v1, /device:TPU:4, one launch (start us, length us, event | category | flops | bytes accessed | tf_op | source)
XLA Modules:
  0.0 473.2 jit_solution(5973791023075451081)
XLA Ops:
  6.5 0.0 all-gather.4.cloned.1.call-start
  6.5 0.7 all-gather.4.cloned.1.call-update
  7.3 0.0 all-gather.6.cloned.1.call-start
  7.3 0.7 all-gather.6.cloned.1.call-update
  8.0 0.0 all-gather.8.cloned.1.call-start
  8.1 0.7 all-gather.8.cloned.1.call-update
  8.7 0.0 reduce-scatter.2.cloned.1.call-start
  8.8 118.9 %all-gather.4.cloned.1.call-done.k_ref = bf16[8192,128]{1,0:T(8,128)(2,1)} async-done(((bf16[128,128]{1,0:T(8,128)(2,1)}), bf16[8192,128]{1,0:T(8,128)(2,1)}) %all-gather.4.cloned.1.call-update) | async-done | bytes 2097168 | tf_op jit(solution)/shard_map/all_gather | solution.py:65
  127.7 106.3 %all-gather.6.cloned.1.call-done.v_ref = bf16[8192,128]{1,0:T(8,128)(2,1)} async-done(((bf16[128,128]{1,0:T(8,128)(2,1)}), bf16[8192,128]{1,0:T(8,128)(2,1)}) %all-gather.6.cloned.1.call-update) | async-done | bytes 2097168 | tf_op jit(solution)/shard_map/all_gather | solution.py:66
  233.9 0.0 copy-start
  233.9 1.6 copy-done
  235.5 0.0 copy-start.1
  235.5 1.6 copy-done.1
  237.1 0.0 copy-start.2
  237.1 0.9 copy-done.2
  238.1 6.4 %shard_map.46 = bf16[128,1024]{1,0:T(8,128)(2,1)S(1)} custom-call(bf16[128,1024]{1,0:T(8,128)(2,1)S(1)} %copy-done.2, bf16[8192,128]{1,0:T(8,128)(2,1)S(1)} %copy-done, bf16[8192,128]{1,0:T(8,128)(2,1)S(1)} %copy-done.1), custom_call_target="tpu_custom_call" | custom-call | flops 4000000000 | bytes 5242880 | tf_op jit(solution)/shard_map/pallas_call | solution.py:68
  244.5 150.0 %all-gather.8.cloned.1.call-done = bf16[4096,1024]{1,0:T(8,128)(2,1)} async-done(((bf16[64,1024]{1,0:T(8,128)(2,1)}), bf16[4096,1024]{1,0:T(8,128)(2,1)}) %all-gather.8.cloned.1.call-update) | async-done | bytes 8388624 | tf_op jit(solution)/shard_map/all_gather | solution.py:67
  394.5 7.3 %convolution_convert_fusion = bf16[128,4096]{1,0:T(8,128)(2,1)} fusion(bf16[128,1024]{1,0:T(8,128)(2,1)S(1)} %shard_map.46, bf16[4096,1024]{1,0:T(8,128)(2,1)} %all-gather.8.cloned.1.call-done), kind=kOutput, calls=%fused_computation | convolution fusion | flops 1074266112 | bytes 9699328 | tf_op jit(solution)/shard_map/dot_general | solution.py:77
  401.8 0.0 reduce-scatter.2.cloned.1.call-update
  401.9 64.8 %reduce-scatter.2.cloned.1.call-done = bf16[128,512]{1,0:T(8,128)(2,1)} async-done(((bf16[128,4096]{1,0:T(8,128)(2,1)}), bf16[128,512]{1,0:T(8,128)(2,1)}) %reduce-scatter.2.cloned.1.call-update) | async-done | bytes 131088 | tf_op jit(solution)/shard_map/reduce_scatter | solution.py:80
Async XLA Ops:
  6.5 121.1 %all-gather.4.cloned.1.call-start = ((), (), s32[]{:S(2)}) async-start(), calls=%async_computation.1 | async-start | bytes 2129920 | tf_op jit(solution)/shard_map/all_gather | solution.py:65
  7.3 226.7 %all-gather.6.cloned.1.call-start = ((), (), s32[]{:S(2)}) async-start(), calls=%async_computation.2 | async-start | bytes 2129920 | tf_op jit(solution)/shard_map/all_gather | solution.py:66
  8.0 386.5 %all-gather.8.cloned.1.call-start = ((), (), s32[]{:S(2)}) async-start(), calls=%async_computation.3 | async-start | bytes 8519680 | tf_op jit(solution)/shard_map/all_gather | solution.py:67
  8.7 457.9 %reduce-scatter.2.cloned.1.call-start = ((), (), s32[]{:S(2)}) async-start(), calls=%async_computation.4 | async-start | bytes 1179648 | tf_op jit(solution)/shard_map/reduce_scatter | solution.py:80
  233.9 1.6 copy-start
  235.5 1.6 copy-start.1
  237.1 0.9 copy-start.2
Sparse Core Ops, SparseCore 0:
  11.8 115.8 all-gather.3
  132.1 101.7 all-gather.5
  238.4 156.0 all-gather.7
  402.0 64.6 reduce-scatter.1

commit v2 on v1

v2 whole, which is shorter than its diff:
```python
import math

import jax
import jax.numpy as jnp
from jax import lax
from jax.experimental import pallas as pl
from jax.experimental.pallas import tpu as pltpu
from jax.sharding import PartitionSpec as P

HD = 128
HEADS = 8
ROWS = 128
BOTH = 2 * ROWS
N = 4
TP = 8
WROWS = 64
F32 = jnp.float32
BF16 = jnp.bfloat16
SCALE = math.log2(math.e) / math.sqrt(HD)
NEG = -1e30
SUB = 2
SUBROWS = BOTH // SUB
KV, KVO, W, WO = range(4)
CROSS_K, CROSS_V, CROSS_W, SIB_Q, SIB_L, SIB_F = range(64, 70)
SIB_O = 70


def kernel(
    q_in, k_in, v_in, w_in, out,
    kbuf, vbuf, wbuf, qbuf, acc, peak, total, obuf, orecv, lbuf, lrecv, abuf,
    up_recv, dn_recv, up_send, dn_send, fin, fsend, frecv,
    ssem, rsem, usem_s, usem_r, dsem_s, dsem_r, lsem,
):
    me = lax.axis_index("ctx")
    tp = lax.axis_index("tp")
    zh = me // 32
    x = (me // 8) % N
    y = (me // 2) % N
    c = me % 2
    xn, xb = (x + 1) % N, (x + N - 1) % N
    yn, yb = (y + 1) % N, (y + N - 1) % N
    x2, y2 = (x + 2) % N, (y + 2) % N

    def at(z, i, j, k):
        return ((z * N + i) * N + j) * 2 + k

    xp, xm = at(zh, xn, y, c), at(zh, xb, y, c)
    yp, ym = at(zh, x, yn, c), at(zh, x, yb, c)
    zz, sib = at(1 - zh, x, y, c), at(zh, x, y, 1 - c)

    barrier = pltpu.get_barrier_semaphore()

    def greet(ctx, t):
        pl.semaphore_signal(barrier, inc=1, device_id=(ctx, t), device_id_type=pl.DeviceIdType.MESH)

    for dev in (xp, xm, yp, ym, zz, sib):
        greet(dev, tp)

    @pl.when(tp > 0)
    def _():
        greet(me, tp - 1)

    @pl.when(tp < TP - 1)
    def _():
        greet(me, tp + 1)

    loads = [
        pltpu.make_async_copy(k_in, kbuf.at[zh, x, y], lsem.at[0]),
        pltpu.make_async_copy(v_in, vbuf.at[zh, x, y], lsem.at[1]),
        pltpu.make_async_copy(w_in, wbuf.at[zh, x, y], lsem.at[2]),
        pltpu.make_async_copy(q_in, qbuf.at[c], lsem.at[3]),
    ]
    for load in loads:
        load.start()
    pl.semaphore_wait(barrier, 6 + (tp > 0).astype(jnp.int32) + (tp < TP - 1).astype(jnp.int32))

    def remote(src, dst, sem, ctx):
        return pltpu.make_async_remote_copy(
            src_ref=src, dst_ref=dst, send_sem=ssem.at[sem], recv_sem=rsem.at[sem],
            device_id=(ctx, tp), device_id_type=pl.DeviceIdType.MESH,
        )

    def got(dst, sem):
        remote(dst, dst, sem, sib).wait_recv()

    def views(inst):
        z = zh if inst in (KV, W) else 1 - zh
        if inst in (KV, KVO):
            return (kbuf, z, 0, ROWS), (vbuf, z, 0, ROWS)
        return (wbuf, z, 0, WROWS // 2), (wbuf, z, WROWS // 2, WROWS // 2)

    def block(view, i, j, part=None):
        buf, z, lo, n = view
        if part is not None:
            n = n // 2
            lo = lo + part * n
        return buf.at[z, i, j, pl.ds(lo, n)]

    everything = pl.ds(0, N)
    low, high = pl.ds(0, N // 2), pl.ds(N // 2, N // 2)

    def sends(inst, stage):
        a, b = views(inst)
        if stage == 0:
            return [
                (block(a, x, y), xp), (block(a, x, y), xm),
                (block(b, x, y), yp), (block(b, x, y), ym),
            ]
        if stage == 1:
            return [
                (block(a, xb, y, 0), xp), (block(a, xn, y, 1), xm),
                (block(b, x, yb, 0), yp), (block(b, x, yn, 1), ym),
            ]
        if stage == 2:
            return [
                (block(a, everything, y), yp), (block(a, everything, y), ym),
                (block(b, x, everything), xp), (block(b, x, everything), xm),
            ]
        return [
            (block(a, low, yb), yp), (block(a, high, yn), ym),
            (block(b, xb, low), xp), (block(b, xn, high), xm),
        ]

    def arrivals(inst, stage):
        a, b = views(inst)
        if stage == 0:
            return [block(a, xb, y), block(a, xn, y), block(b, x, yb), block(b, x, yn)]
        if stage == 1:
            return [block(a, x2, y, 0), block(a, x2, y, 1), block(b, x, y2, 0), block(b, x, y2, 1)]
        if stage == 2:
            return [
                block(a, everything, yb), block(a, everything, yn),
                block(b, xb, everything), block(b, xn, everything),
            ]
        return [block(a, low, y2), block(a, high, y2), block(b, x2, low), block(b, x2, high)]

    def event(inst, stage):
        base = inst * 16
        if stage > 0:
            for i, dst in enumerate(arrivals(inst, stage - 1)):
                got(dst, base + (stage - 1) * 4 + i)
        if stage < 4:
            for i, (ref, dev) in enumerate(sends(inst, stage)):
                remote(ref, ref, base + stage * 4 + i, dev).start()

    def drain(inst):
        for stage in range(4):
            for i, (ref, dev) in enumerate(sends(inst, stage)):
                remote(ref, ref, inst * 16 + stage * 4 + i, dev).wait_send()

    loads[0].wait()
    loads[1].wait()
    event(KV, 0)

    @pl.when(zh == 0)
    def _():
        remote(kbuf.at[zh, x, y], kbuf.at[zh, x, y], CROSS_K, zz).start()
        remote(vbuf.at[zh, x, y], vbuf.at[zh, x, y], CROSS_V, zz).start()

    loads[3].wait()
    remote(qbuf.at[c], qbuf.at[c], SIB_Q, sib).start()
    loads[2].wait()
    remote(wbuf.at[zh, x, y], wbuf.at[zh, x, y], CROSS_W, zz).start()
    event(W, 0)
    event(KV, 1)
    event(KV, 2)
    event(W, 1)
    event(KV, 3)
    event(W, 2)
    event(KV, 4)
    got(qbuf.at[1 - c], SIB_Q)

    @pl.when(zh == 1)
    def _():
        got(kbuf.at[1 - zh, x, y], CROSS_K)
        got(vbuf.at[1 - zh, x, y], CROSS_V)
        event(KVO, 0)

    keys = N * N * ROWS

    def scores(h, z):
        cols = pl.ds(pl.multiple_of(h * HD, HD), HD)
        q = qbuf[:, :, cols].reshape(BOTH, HD)
        k = kbuf[z].reshape(keys, HD)
        return lax.dot_general(q, k, (((1,), (1,)), ((), ())), preferred_element_type=F32)

    def weigh(s, z):
        m = jnp.max(s, axis=1, keepdims=True) * SCALE
        p = jnp.exp2(s * SCALE - m)
        v = vbuf[z].reshape(keys, HD)
        v = jnp.concatenate([v, jnp.ones_like(v)], axis=1)
        pv = jnp.dot(p.astype(BF16), v, preferred_element_type=F32)
        return jnp.broadcast_to(m, (BOTH, HD)), pv[:, :HD], pv[:, HD:]

    def finish(h):
        value = acc[h] / total[h]
        acc[h] = value
        obuf[h] = value.astype(BF16)
        lane = lax.broadcasted_iota(jnp.int32, (BOTH, HD), 1)
        lbuf[...] = jnp.where(lane == h, peak[h] + jnp.log2(total[h]), lbuf[...])
        oremote(h).start()

    def oremote(h):
        return pltpu.make_async_remote_copy(
            src_ref=obuf.at[h], dst_ref=orecv.at[h], send_sem=ssem.at[SIB_O + h], recv_sem=rsem.at[SIB_O + h],
            device_id=(sib, tp), device_id_type=pl.DeviceIdType.MESH,
        )

    def at_head(h, k, inst, stage):
        @pl.when(h == k)
        def _():
            event(inst, stage)

    lbuf[...] = jnp.zeros((BOTH, HD), F32)

    @pl.loop(0, HEADS)
    def _(h):
        s = scores(h, zh)
        row = lax.broadcasted_iota(jnp.int32, (BOTH, keys), 0) + (x * N + y) * BOTH
        col = lax.broadcasted_iota(jnp.int32, (BOTH, keys), 1)
        place = (col // ROWS) * BOTH + c * ROWS + col % ROWS
        s = jnp.where(place <= row, s, NEG)
        peak[h], acc[h], total[h] = weigh(s, zh)

        @pl.when(zh == 0)
        def _():
            finish(h)

        @pl.when(zh == 1)
        def _():
            at_head(h, 0, KVO, 1)
            at_head(h, 2, KVO, 2)
            at_head(h, 4, KVO, 3)

        at_head(h, 3, W, 3)
        at_head(h, 6, W, 4)

    got(wbuf.at[1 - zh, x, y], CROSS_W)
    event(WO, 0)

    @pl.when(zh == 0)
    def _():
        event(WO, 1)
        event(WO, 2)
        event(WO, 3)

    @pl.when(zh == 1)
    def _():
        event(KVO, 4)

        @pl.loop(0, HEADS)
        def _(h):
            m, pv, n = weigh(scores(h, 1 - zh), 1 - zh)
            old = peak[h]
            new = jnp.maximum(old, m)
            mine, theirs = jnp.exp2(old - new), jnp.exp2(m - new)
            acc[h] = acc[h] * mine + pv * theirs
            total[h] = total[h] * mine + n * theirs
            peak[h] = new
            finish(h)
            at_head(h, 0, WO, 1)
            at_head(h, 1, WO, 2)
            at_head(h, 5, WO, 3)

    lsend = pltpu.make_async_remote_copy(
        src_ref=lbuf, dst_ref=lrecv, send_sem=ssem.at[SIB_L], recv_sem=rsem.at[SIB_L],
        device_id=(sib, tp), device_id_type=pl.DeviceIdType.MESH,
    )
    lsend.start()
    lsend.wait_recv()
    for h in range(HEADS):
        oremote(h).wait_recv()
        share = 1.0 / (1.0 + jnp.exp2(lrecv[:, h : h + 1] - lbuf[:, h : h + 1]))
        other = orecv[h].astype(F32)
        abuf[:, h * HD : (h + 1) * HD] = (other + (acc[h] - other) * share).astype(BF16)

    event(WO, 4)

    def product(d):
        weight = wbuf[d // N, d % N].reshape(N * WROWS, HEADS * HD)
        return lax.dot_general(
            abuf[...], weight, (((1,), (1,)), ((), ())), preferred_element_type=F32
        )

    def hop(d, i, send, recv, s_sem, r_sem, to):
        rows = pl.ds(i * SUBROWS, SUBROWS)
        return pltpu.make_async_remote_copy(
            src_ref=send.at[d, rows], dst_ref=recv.at[d, rows],
            send_sem=s_sem.at[d, i], recv_sem=r_sem.at[d, i],
            device_id=(me, to), device_id_type=pl.DeviceIdType.MESH,
        )

    def up(d, i):
        return hop(d, i, up_send, up_recv, usem_s, usem_r, jnp.minimum(tp + 1, TP - 1))

    def down(d, i):
        return hop(d, i, dn_send, dn_recv, dsem_s, dsem_r, jnp.maximum(tp - 1, 0))

    @pl.loop(0, TP - 1)
    def _(k):
        d = TP - 1 - k

        @pl.when(tp < d)
        def _():
            fin[...] = product(d)
            for i in range(SUB):
                rows = slice(i * SUBROWS, (i + 1) * SUBROWS)

                @pl.when(tp > 0)
                def _():
                    up(d, i).wait_recv()
                    up_send[d, rows] = (fin[rows] + up_recv[d, rows].astype(F32)).astype(BF16)

                @pl.when(tp == 0)
                def _():
                    up_send[d, rows] = fin[rows].astype(BF16)

                up(d, i).start()

        @pl.when(tp > k)
        def _():
            fin[...] = product(k)
            for i in range(SUB):
                rows = slice(i * SUBROWS, (i + 1) * SUBROWS)

                @pl.when(tp < TP - 1)
                def _():
                    down(k, i).wait_recv()
                    dn_send[k, rows] = (fin[rows] + dn_recv[k, rows].astype(F32)).astype(BF16)

                @pl.when(tp == TP - 1)
                def _():
                    dn_send[k, rows] = fin[rows].astype(BF16)

                down(k, i).start()

    fin[...] = product(tp)

    @pl.when(tp > 0)
    def _():
        for i in range(SUB):
            up(tp, i).wait_recv()
        fin[...] += up_recv[tp].astype(F32)

    @pl.when(tp < TP - 1)
    def _():
        for i in range(SUB):
            down(tp, i).wait_recv()
        fin[...] += dn_recv[tp].astype(F32)

    def half(k):
        return fin[pl.ds(pl.multiple_of(k * ROWS, ROWS), ROWS), :].astype(BF16)

    fsend[...] = half(1 - c)
    frecv[c] = half(c)
    last = remote(fsend, frecv.at[c], SIB_F, sib)
    last.start()
    got(frecv.at[1 - c], SIB_F)
    for j in range(N):
        cols = slice(j * WROWS, (j + 1) * WROWS)
        out[:, j * 2 * WROWS : (j + 1) * 2 * WROWS] = jnp.concatenate(
            [frecv[0, :, cols], frecv[1, :, cols]], axis=1
        )

    last.wait_send()
    lsend.wait_send()
    for h in range(HEADS):
        oremote(h).wait_send()
    for inst in (KV, W, WO):
        drain(inst)

    @pl.when(zh == 1)
    def _():
        drain(KVO)

    @pl.when(zh == 0)
    def _():
        remote(kbuf.at[zh, x, y], kbuf.at[zh, x, y], CROSS_K, zz).wait_send()
        remote(vbuf.at[zh, x, y], vbuf.at[zh, x, y], CROSS_V, zz).wait_send()

    remote(wbuf.at[zh, x, y], wbuf.at[zh, x, y], CROSS_W, zz).wait_send()
    remote(qbuf.at[c], qbuf.at[c], SIB_Q, sib).wait_send()

    @pl.loop(0, TP - 1)
    def _(k):
        d = TP - 1 - k

        @pl.when(tp < d)
        def _():
            for i in range(SUB):
                up(d, i).wait_send()

        @pl.when(tp > k)
        def _():
            for i in range(SUB):
                down(k, i).wait_send()


def body(queries, keys, values, out_weight):
    slab = (2, N, N)
    sums = (TP, BOTH, BOTH)
    return pl.pallas_call(
        kernel,
        out_shape=jax.ShapeDtypeStruct((ROWS, TP * WROWS), BF16),
        in_specs=[pl.BlockSpec(memory_space=pl.ANY)] * 4,
        out_specs=pl.BlockSpec(memory_space=pltpu.VMEM),
        scratch_shapes=[
            pltpu.VMEM(slab + (ROWS, HD), BF16),
            pltpu.VMEM(slab + (ROWS, HD), BF16),
            pltpu.VMEM(slab + (WROWS, HEADS * HD), BF16),
            pltpu.VMEM((2, ROWS, HEADS * HD), BF16),
            pltpu.VMEM((HEADS, BOTH, HD), F32),
            pltpu.VMEM((HEADS, BOTH, HD), F32),
            pltpu.VMEM((HEADS, BOTH, HD), F32),
            pltpu.VMEM((HEADS, BOTH, HD), BF16),
            pltpu.VMEM((HEADS, BOTH, HD), BF16),
            pltpu.VMEM((BOTH, HD), F32),
            pltpu.VMEM((BOTH, HD), F32),
            pltpu.VMEM((BOTH, HEADS * HD), BF16),
            pltpu.VMEM(sums, BF16),
            pltpu.VMEM(sums, BF16),
            pltpu.VMEM(sums, BF16),
            pltpu.VMEM(sums, BF16),
            pltpu.VMEM((BOTH, BOTH), F32),
            pltpu.VMEM((ROWS, BOTH), BF16),
            pltpu.VMEM((2, ROWS, BOTH), BF16),
            pltpu.SemaphoreType.DMA((78,)),
            pltpu.SemaphoreType.DMA((78,)),
            pltpu.SemaphoreType.DMA((TP, SUB)),
            pltpu.SemaphoreType.DMA((TP, SUB)),
            pltpu.SemaphoreType.DMA((TP, SUB)),
            pltpu.SemaphoreType.DMA((TP, SUB)),
            pltpu.SemaphoreType.DMA((4,)),
        ],
        compiler_params=pltpu.CompilerParams(
            collective_id=0, has_side_effects=True, vmem_limit_bytes=56 * 2**20
        ),
        cost_estimate=pl.CostEstimate(flops=5 * 10**9, bytes_accessed=2**20, transcendentals=0),
    )(queries, keys, values, out_weight)


def solution(mesh):
    return jax.shard_map(
        body,
        mesh=mesh,
        in_specs=(P("ctx", "tp"), P("ctx", "tp"), P("ctx", "tp"), P("ctx", "tp")),
        out_specs=P("ctx", "tp"),
        check_vma=False,
    )
```

time: 473 us -> 153 us (0.32)
  the two profiles are of different devices: /device:TPU:4 before, /device:TPU:385 now
where the time goes in v2:
time: 153 us
  Pallas kernels  151 us (99%)
  local copies, waits for them, and re-layouts  1.57 us (1%)
    pallas_call x1, Pallas kernels, body(): pl.pallas_call(kernel, out_shape=jax.ShapeDtypeStruct((ROWS, TP * WROWS),...  151 us

profile of v2, /device:TPU:385, one launch (start us, length us, event | category | flops | bytes accessed | tf_op | source)
XLA Modules:
  0.0 152.8 jit_solution(4081387466337435445)
XLA Ops:
  0.0 151.2 %shard_map.46 = bf16[128,512]{1,0:T(8,128)(2,1)} custom-call(bf16[128,1024]{1,0:T(8,128)(2,1)} %q_in.1, bf16[128,128]{1,0:T(8,128)(2,1)} %k_in.1, bf16[128,128]{1,0:T(8,128)(2,1)} %v_in.1, bf16[64,1024]{1,0:T(8,128)(2,1)} %w_in.1), custom_call_target="tpu_custom_call" | custom-call | flops 5000000000 | bytes 1048576 | tf_op jit(solution)/shard_map/pallas_call | solution.py:402
  151.2 1.6 %copy.6 = bf16[128,512]{1,0:T(8,128)(2,1)} copy(bf16[128,512]{1,0:T(8,128)(2,1)} %shard_map.46) | data formatting | bytes 262144

commit v3 on v2

--- a/solution.py
+++ b/solution.py
@@ -14,21 +14,30 @@
 N = 4
 TP = 8
 WROWS = 64
+PIECE = WROWS // 2
 F32 = jnp.float32
 BF16 = jnp.bfloat16
 SCALE = math.log2(math.e) / math.sqrt(HD)
 NEG = -1e30
-SUB = 2
+SUB = 4
+HALF = SUB // 2
 SUBROWS = BOTH // SUB
-KV, KVO, W, WO = range(4)
-CROSS_K, CROSS_V, CROSS_W, SIB_Q, SIB_L, SIB_F = range(64, 70)
-SIB_O = 70
+KV, KVO, WA, WB, OA, OB = range(6)
+BEFORE = [(KV, 0), (WA, 0), (WB, 0), (KV, 1), (WA, 1), (KV, 2), (WB, 1), (KV, 3)]
+FIRST_HALF = {0: [(OA, 0), (WA, 2)], 2: [(WB, 2)], 3: [(OA, 1)], 4: [(OB, 0)], 7: [(OB, 1)]}
+FIRST_HALF_END = [(OA, 2), (OB, 2)]
+LAST_HALF_BEGIN = [(KVO, 0)]
+LAST_HALF = {0: [(WA, 2)], 2: [(KVO, 1)], 4: [(WB, 2)], 5: [(OA, 0)]}
+LAST_HALF_MIDDLE = [(KVO, 2)]
+LAST_HALF_MORE = {0: [(OB, 0), (OA, 1)], 3: [(OB, 1)], 4: [(OA, 2)], 6: [(OB, 2)]}
+AFTER = [(WA, 3), (WB, 3), (OA, 3), (OB, 3)]
+CROSS_K, CROSS_V, CROSS_W, SIB_Q, SIB_L, SIB_O, SIB_F = 96, 97, 98, 100, 101, 102, 110
 
 
 def kernel(
     q_in, k_in, v_in, w_in, out,
     kbuf, vbuf, wbuf, qbuf, acc, peak, total, obuf, orecv, lbuf, lrecv, abuf,
-    up_recv, dn_recv, up_send, dn_send, fin, fsend, frecv,
+    up_recv, dn_recv, up_send, dn_send, prod, fsend, frecv,
     ssem, rsem, usem_s, usem_r, dsem_s, dsem_r, lsem,
 ):
     me = lax.axis_index("ctx")
@@ -46,6 +55,7 @@
 
     xp, xm = at(zh, xn, y, c), at(zh, xb, y, c)
     yp, ym = at(zh, x, yn, c), at(zh, x, yb, c)
+    xq, yq = at(zh, x2, y, c), at(zh, x, y2, c)
     zz, sib = at(1 - zh, x, y, c), at(zh, x, y, 1 - c)
 
     barrier = pltpu.get_barrier_semaphore()
@@ -53,7 +63,7 @@
     def greet(ctx, t):
         pl.semaphore_signal(barrier, inc=1, device_id=(ctx, t), device_id_type=pl.DeviceIdType.MESH)
 
-    for dev in (xp, xm, yp, ym, zz, sib):
+    for dev in (xp, xm, xq, yp, ym, yq, zz, sib):
         greet(dev, tp)
 
     @pl.when(tp > 0)
@@ -72,7 +82,7 @@
     ]
     for load in loads:
         load.start()
-    pl.semaphore_wait(barrier, 6 + (tp > 0).astype(jnp.int32) + (tp < TP - 1).astype(jnp.int32))
+    pl.semaphore_wait(barrier, 8 + (tp > 0).astype(jnp.int32) + (tp < TP - 1).astype(jnp.int32))
 
     def remote(src, dst, sem, ctx):
         return pltpu.make_async_remote_copy(
@@ -84,16 +94,14 @@
         remote(dst, dst, sem, sib).wait_recv()
 
     def views(inst):
-        z = zh if inst in (KV, W) else 1 - zh
+        z = zh if inst in (KV, WA, WB) else 1 - zh
         if inst in (KV, KVO):
             return (kbuf, z, 0, ROWS), (vbuf, z, 0, ROWS)
-        return (wbuf, z, 0, WROWS // 2), (wbuf, z, WROWS // 2, WROWS // 2)
-
-    def block(view, i, j, part=None):
+        lo, n = (0 if inst in (WA, OA) else PIECE), PIECE // 2
+        return (wbuf, z, lo, n), (wbuf, z, lo + n, n)
+
+    def block(view, i, j):
         buf, z, lo, n = view
-        if part is not None:
-            n = n // 2
-            lo = lo + part * n
         return buf.at[z, i, j, pl.ds(lo, n)]
 
     everything = pl.ds(0, N)
@@ -102,20 +110,19 @@
     def sends(inst, stage):
         a, b = views(inst)
         if stage == 0:
-            return [
-                (block(a, x, y), xp), (block(a, x, y), xm),
-                (block(b, x, y), yp), (block(b, x, y), ym),
+            return [(block(a, x, y), dev) for dev in (xp, xm, xq)] + [
+                (block(b, x, y), dev) for dev in (yp, ym, yq)
+            ]
+        if inst == KVO and stage == 1:
+            return [(block(a, everything, y), dev) for dev in (yp, ym, yq)] + [
+                (block(b, x, everything), dev) for dev in (xp, xm, xq)
             ]
         if stage == 1:
-            return [
-                (block(a, xb, y, 0), xp), (block(a, xn, y, 1), xm),
-                (block(b, x, yb, 0), yp), (block(b, x, yn, 1), ym),
+            return [(block(a, everything, y), dev) for dev in (yp, ym)] + [
+                (block(b, x, everything), dev) for dev in (xp, xm)
             ]
-        if stage == 2:
-            return [
-                (block(a, everything, y), yp), (block(a, everything, y), ym),
-                (block(b, x, everything), xp), (block(b, x, everything), xm),
-            ]
+        if inst == KVO or stage == 3:
+            return []
         return [
             (block(a, low, yb), yp), (block(a, high, yn), ym),
             (block(b, xb, low), xp), (block(b, xn, high), xm),
@@ -124,13 +131,14 @@
     def arrivals(inst, stage):
         a, b = views(inst)
         if stage == 0:
-            return [block(a, xb, y), block(a, xn, y), block(b, x, yb), block(b, x, yn)]
+            return [block(a, i, y) for i in (xb, xn, x2)] + [block(b, x, j) for j in (yb, yn, y2)]
+        if inst == KVO:
+            return [block(a, everything, j) for j in (yb, yn, y2)] + [
+                block(b, i, everything) for i in (xb, xn, x2)
+            ]
         if stage == 1:
-            return [block(a, x2, y, 0), block(a, x2, y, 1), block(b, x, y2, 0), block(b, x, y2, 1)]
-        if stage == 2:
-            return [
-                block(a, everything, yb), block(a, everything, yn),
-                block(b, xb, everything), block(b, xn, everything),
+            return [block(a, everything, j) for j in (yb, yn)] + [
+                block(b, i, everything) for i in (xb, xn)
             ]
         return [block(a, low, y2), block(a, high, y2), block(b, x2, low), block(b, x2, high)]
 
@@ -138,43 +146,41 @@
         base = inst * 16
         if stage > 0:
             for i, dst in enumerate(arrivals(inst, stage - 1)):
-                got(dst, base + (stage - 1) * 4 + i)
-        if stage < 4:
+                got(dst, base + (stage - 1) * 6 + i)
+        elif inst == KVO:
+            got(kbuf.at[1 - zh, x, y], CROSS_K)
+            got(vbuf.at[1 - zh, x, y], CROSS_V)
+        elif inst in (OA, OB):
+            i = inst - OA
+            got(wbuf.at[1 - zh, x, y, pl.ds(i * PIECE, PIECE)], CROSS_W + i)
+        for i, (ref, dev) in enumerate(sends(inst, stage)):
+            remote(ref, ref, base + stage * 6 + i, dev).start()
+
+    def drain(inst):
+        for stage in range(3):
             for i, (ref, dev) in enumerate(sends(inst, stage)):
-                remote(ref, ref, base + stage * 4 + i, dev).start()
-
-    def drain(inst):
-        for stage in range(4):
-            for i, (ref, dev) in enumerate(sends(inst, stage)):
-                remote(ref, ref, inst * 16 + stage * 4 + i, dev).wait_send()
+                remote(ref, ref, inst * 16 + stage * 6 + i, dev).wait_send()
+
+    def cross(i):
+        ref = wbuf.at[zh, x, y, pl.ds(i * PIECE, PIECE)]
+        return remote(ref, ref, CROSS_W + i, zz)
 
     loads[0].wait()
     loads[1].wait()
-    event(KV, 0)
 
     @pl.when(zh == 0)
     def _():
         remote(kbuf.at[zh, x, y], kbuf.at[zh, x, y], CROSS_K, zz).start()
         remote(vbuf.at[zh, x, y], vbuf.at[zh, x, y], CROSS_V, zz).start()
 
+    loads[2].wait()
+    cross(0).start()
+    cross(1).start()
     loads[3].wait()
     remote(qbuf.at[c], qbuf.at[c], SIB_Q, sib).start()
-    loads[2].wait()
-    remote(wbuf.at[zh, x, y], wbuf.at[zh, x, y], CROSS_W, zz).start()
-    event(W, 0)
-    event(KV, 1)
-    event(KV, 2)
-    event(W, 1)
-    event(KV, 3)
-    event(W, 2)
-    event(KV, 4)
+    for one in BEFORE:
+        event(*one)
     got(qbuf.at[1 - c], SIB_Q)
-
-    @pl.when(zh == 1)
-    def _():
-        got(kbuf.at[1 - zh, x, y], CROSS_K)
-        got(vbuf.at[1 - zh, x, y], CROSS_V)
-        event(KVO, 0)
 
     keys = N * N * ROWS
 
@@ -206,12 +212,20 @@
             device_id=(sib, tp), device_id_type=pl.DeviceIdType.MESH,
         )
 
-    def at_head(h, k, inst, stage):
-        @pl.when(h == k)
-        def _():
-            event(inst, stage)
+    def at_head(h, table):
+        for k, events in table.items():
+
+            @pl.when(h == k)
+            def _():
+                for one in events:
+                    event(*one)
 
     lbuf[...] = jnp.zeros((BOTH, HD), F32)
+
+    @pl.when(zh == 1)
+    def _():
+        for one in LAST_HALF_BEGIN:
+            event(*one)
 
     @pl.loop(0, HEADS)
     def _(h):
@@ -225,28 +239,21 @@
         @pl.when(zh == 0)
         def _():
             finish(h)
+            at_head(h, FIRST_HALF)
 
         @pl.when(zh == 1)
         def _():
-            at_head(h, 0, KVO, 1)
-            at_head(h, 2, KVO, 2)
-            at_head(h, 4, KVO, 3)
-
-        at_head(h, 3, W, 3)
-        at_head(h, 6, W, 4)
-
-    got(wbuf.at[1 - zh, x, y], CROSS_W)
-    event(WO, 0)
+            at_head(h, LAST_HALF)
 
     @pl.when(zh == 0)
     def _():
-        event(WO, 1)
-        event(WO, 2)
-        event(WO, 3)
+        for one in FIRST_HALF_END:
+            event(*one)
 
     @pl.when(zh == 1)
     def _():
-        event(KVO, 4)
+        for one in LAST_HALF_MIDDLE:
+            event(*one)
 
         @pl.loop(0, HEADS)
         def _(h):
@@ -258,9 +265,7 @@
             total[h] = total[h] * mine + n * theirs
             peak[h] = new
             finish(h)
-            at_head(h, 0, WO, 1)
-            at_head(h, 1, WO, 2)
-            at_head(h, 5, WO, 3)
+            at_head(h, LAST_HALF_MORE)
 
     lsend = pltpu.make_async_remote_copy(
         src_ref=lbuf, dst_ref=lrecv, send_sem=ssem.at[SIB_L], recv_sem=rsem.at[SIB_L],
@@ -274,7 +279,8 @@
         other = orecv[h].astype(F32)
         abuf[:, h * HD : (h + 1) * HD] = (other + (acc[h] - other) * share).astype(BF16)
 
-    event(WO, 4)
+    for one in AFTER:
+        event(*one)
 
     def product(d):
         weight = wbuf[d // N, d % N].reshape(N * WROWS, HEADS * HD)
@@ -282,8 +288,12 @@
             abuf[...], weight, (((1,), (1,)), ((), ())), preferred_element_type=F32
         )
 
+    def sub(i):
+        first = (1 - c) if i < HALF else c
+        return pl.ds(pl.multiple_of(first * ROWS + (i % HALF) * SUBROWS, SUBROWS), SUBROWS)
+
     def hop(d, i, send, recv, s_sem, r_sem, to):
-        rows = pl.ds(i * SUBROWS, SUBROWS)
+        rows = sub(i)
         return pltpu.make_async_remote_copy(
             src_ref=send.at[d, rows], dst_ref=recv.at[d, rows],
             send_sem=s_sem.at[d, i], recv_sem=r_sem.at[d, i],
@@ -297,76 +307,86 @@
         return hop(d, i, dn_send, dn_recv, dsem_s, dsem_r, jnp.maximum(tp - 1, 0))
 
     @pl.loop(0, TP - 1)
-    def _(k):
-        d = TP - 1 - k
-
-        @pl.when(tp < d)
-        def _():
-            fin[...] = product(d)
-            for i in range(SUB):
-                rows = slice(i * SUBROWS, (i + 1) * SUBROWS)
-
+    def _(u):
+        above = TP - 1 - u + tp
+        below = u - TP + 1 + tp
+
+        @pl.when(u >= tp)
+        def _():
+            prod[above] = product(above)
+
+        @pl.when(below >= 0)
+        def _():
+            prod[below] = product(below)
+
+        for i in range(SUB):
+            rows = sub(i)
+
+            @pl.when(u >= tp)
+            def _():
                 @pl.when(tp > 0)
                 def _():
-                    up(d, i).wait_recv()
-                    up_send[d, rows] = (fin[rows] + up_recv[d, rows].astype(F32)).astype(BF16)
+                    up(above, i).wait_recv()
+                    up_send[above, rows] = (prod[above, rows] + up_recv[above, rows].astype(F32)).astype(BF16)
 
                 @pl.when(tp == 0)
                 def _():
-                    up_send[d, rows] = fin[rows].astype(BF16)
-
-                up(d, i).start()
-
-        @pl.when(tp > k)
-        def _():
-            fin[...] = product(k)
-            for i in range(SUB):
-                rows = slice(i * SUBROWS, (i + 1) * SUBROWS)
-
+                    up_send[above, rows] = prod[above, rows].astype(BF16)
+
+                up(above, i).start()
+
+            @pl.when(below >= 0)
+            def _():
                 @pl.when(tp < TP - 1)
                 def _():
-                    down(k, i).wait_recv()
-                    dn_send[k, rows] = (fin[rows] + dn_recv[k, rows].astype(F32)).astype(BF16)
+                    down(below, i).wait_recv()
+                    dn_send[below, rows] = (prod[below, rows] + dn_recv[below, rows].astype(F32)).astype(BF16)
 
                 @pl.when(tp == TP - 1)
                 def _():
-                    dn_send[k, rows] = fin[rows].astype(BF16)
-
-                down(k, i).start()
-
-    fin[...] = product(tp)
-
-    @pl.when(tp > 0)
-    def _():
-        for i in range(SUB):
+                    dn_send[below, rows] = prod[below, rows].astype(BF16)
+
+                down(below, i).start()
+
+    prod[tp] = product(tp)
+
+    def last(i):
+        rows = pl.ds((i % HALF) * SUBROWS, SUBROWS)
+        return remote(fsend.at[rows], frecv.at[c, rows], SIB_F + i, sib)
+
+    for i in range(SUB):
+        rows = sub(i)
+
+        @pl.when(tp > 0)
+        def _():
             up(tp, i).wait_recv()
-        fin[...] += up_recv[tp].astype(F32)
-
-    @pl.when(tp < TP - 1)
-    def _():
-        for i in range(SUB):
+            prod[tp, rows] += up_recv[tp, rows].astype(F32)
+
+        @pl.when(tp < TP - 1)
+        def _():
             down(tp, i).wait_recv()
-        fin[...] += dn_recv[tp].astype(F32)
-
-    def half(k):
-        return fin[pl.ds(pl.multiple_of(k * ROWS, ROWS), ROWS), :].astype(BF16)
-
-    fsend[...] = half(1 - c)
-    frecv[c] = half(c)
-    last = remote(fsend, frecv.at[c], SIB_F, sib)
-    last.start()
-    got(frecv.at[1 - c], SIB_F)
+            prod[tp, rows] += dn_recv[tp, rows].astype(F32)
+
+        part = pl.ds((i % HALF) * SUBROWS, SUBROWS)
+        if i < HALF:
+            fsend[part] = prod[tp, rows].astype(BF16)
+            last(i).start()
+        else:
+            frecv[c, part] = prod[tp, rows].astype(BF16)
+    for i in range(HALF):
+        got(frecv.at[1 - c, pl.ds(i * SUBROWS, SUBROWS)], SIB_F + i)
     for j in range(N):
         cols = slice(j * WROWS, (j + 1) * WROWS)
         out[:, j * 2 * WROWS : (j + 1) * 2 * WROWS] = jnp.concatenate(
             [frecv[0, :, cols], frecv[1, :, cols]], axis=1
         )
 
-    last.wait_send()
+    for i in range(HALF):
+        last(i).wait_send()
     lsend.wait_send()
     for h in range(HEADS):
         oremote(h).wait_send()
-    for inst in (KV, W, WO):
+    for inst in (KV, WA, WB, OA, OB):
         drain(inst)
 
     @pl.when(zh == 1)
@@ -378,7 +398,8 @@
         remote(kbuf.at[zh, x, y], kbuf.at[zh, x, y], CROSS_K, zz).wait_send()
         remote(vbuf.at[zh, x, y], vbuf.at[zh, x, y], CROSS_V, zz).wait_send()
 
-    remote(wbuf.at[zh, x, y], wbuf.at[zh, x, y], CROSS_W, zz).wait_send()
+    cross(0).wait_send()
+    cross(1).wait_send()
     remote(qbuf.at[c], qbuf.at[c], SIB_Q, sib).wait_send()
 
     @pl.loop(0, TP - 1)
@@ -421,11 +442,11 @@
             pltpu.VMEM(sums, BF16),
             pltpu.VMEM(sums, BF16),
             pltpu.VMEM(sums, BF16),
-            pltpu.VMEM((BOTH, BOTH), F32),
+            pltpu.VMEM(sums, F32),
             pltpu.VMEM((ROWS, BOTH), BF16),
             pltpu.VMEM((2, ROWS, BOTH), BF16),
-            pltpu.SemaphoreType.DMA((78,)),
-            pltpu.SemaphoreType.DMA((78,)),
+            pltpu.SemaphoreType.DMA((SIB_F + HALF,)),
+            pltpu.SemaphoreType.DMA((SIB_F + HALF,)),
             pltpu.SemaphoreType.DMA((TP, SUB)),
             pltpu.SemaphoreType.DMA((TP, SUB)),
             pltpu.SemaphoreType.DMA((TP, SUB)),

time: 153 us -> 84.6 us (0.55)
  the two profiles are of different devices: /device:TPU:385 before, /device:TPU:1 now
where the time goes in v3:
time: 84.6 us; the launch traced here: 84.4 us
  Pallas kernels  82.9 us (98%)
  local copies, waits for them, and re-layouts  1.57 us (2%)
    pallas_call x1, Pallas kernels, body(): pl.pallas_call(kernel, out_shape=jax.ShapeDtypeStruct((ROWS, TP * WROWS),...  82.9 us

profile of v3, /device:TPU:1, one launch (start us, length us, event | category | flops | bytes accessed | tf_op | source)
XLA Modules:
  0.0 84.4 jit_solution(14980956309471526757)
XLA Ops:
  0.0 82.9 %shard_map.46 = bf16[128,512]{1,0:T(8,128)(2,1)} custom-call(bf16[128,1024]{1,0:T(8,128)(2,1)} %q_in.1, bf16[128,128]{1,0:T(8,128)(2,1)} %k_in.1, bf16[128,128]{1,0:T(8,128)(2,1)} %v_in.1, bf16[64,1024]{1,0:T(8,128)(2,1)} %w_in.1), custom_call_target="tpu_custom_call" | custom-call | flops 5000000000 | bytes 1048576 | tf_op jit(solution)/shard_map/pallas_call | solution.py:423
  82.9 1.6 %copy.6 = bf16[128,512]{1,0:T(8,128)(2,1)} copy(bf16[128,512]{1,0:T(8,128)(2,1)} %shard_map.46) | data formatting | bytes 262144

commit v4 on v3

--- a/solution.py
+++ b/solution.py
@@ -19,18 +19,22 @@
 BF16 = jnp.bfloat16
 SCALE = math.log2(math.e) / math.sqrt(HD)
 NEG = -1e30
-SUB = 4
-HALF = SUB // 2
+SUB = 2
 SUBROWS = BOTH // SUB
+PARTS = 2
+COLS = BOTH // PARTS
 KV, KVO, WA, WB, OA, OB = range(6)
-BEFORE = [(KV, 0), (WA, 0), (WB, 0), (KV, 1), (WA, 1), (KV, 2), (WB, 1), (KV, 3)]
+BEFORE = [(WA, 0), (WB, 0), (KV, 1), (WA, 1)]
+BEFORE_MORE = [(KV, 2), (WB, 1), (KV, 3)]
 FIRST_HALF = {0: [(OA, 0), (WA, 2)], 2: [(WB, 2)], 3: [(OA, 1)], 4: [(OB, 0)], 7: [(OB, 1)]}
-FIRST_HALF_END = [(OA, 2), (OB, 2)]
+FIRST_HALF_END = []
 LAST_HALF_BEGIN = [(KVO, 0)]
-LAST_HALF = {0: [(WA, 2)], 2: [(KVO, 1)], 4: [(WB, 2)], 5: [(OA, 0)]}
-LAST_HALF_MIDDLE = [(KVO, 2)]
-LAST_HALF_MORE = {0: [(OB, 0), (OA, 1)], 3: [(OB, 1)], 4: [(OA, 2)], 6: [(OB, 2)]}
-AFTER = [(WA, 3), (WB, 3), (OA, 3), (OB, 3)]
+LAST_HALF = {0:[(WA,2)],1:[(WB,2)],2:[(KVO,1)],5:[(OA,0)],6:[(OB,0)]}
+LAST_HALF_MIDDLE = [(OA,1),(KVO,2)]
+LAST_HALF_MORE = {0:[(OB,1)],3:[(OA,2)],5:[(OB,2)]}
+AFTER = [(WA, 3), (WB, 3)]
+DURING = {1: [(OA, 2)], 2: [(OB, 2)]}
+LAST = [(OA, 3), (OB, 3)]
 CROSS_K, CROSS_V, CROSS_W, SIB_Q, SIB_L, SIB_O, SIB_F = 96, 97, 98, 100, 101, 102, 110
 
 
@@ -173,12 +177,25 @@
         remote(kbuf.at[zh, x, y], kbuf.at[zh, x, y], CROSS_K, zz).start()
         remote(vbuf.at[zh, x, y], vbuf.at[zh, x, y], CROSS_V, zz).start()
 
+    event(KV, 0)
     loads[2].wait()
-    cross(0).start()
-    cross(1).start()
+
+    @pl.when(zh == 0)
+    def _():
+        cross(0).start()
+        cross(1).start()
+
     loads[3].wait()
     remote(qbuf.at[c], qbuf.at[c], SIB_Q, sib).start()
     for one in BEFORE:
+        event(*one)
+
+    @pl.when(zh == 1)
+    def _():
+        cross(0).start()
+        cross(1).start()
+
+    for one in BEFORE_MORE:
         event(*one)
     got(qbuf.at[1 - c], SIB_Q)
 
@@ -279,116 +296,139 @@
         other = orecv[h].astype(F32)
         abuf[:, h * HD : (h + 1) * HD] = (other + (acc[h] - other) * share).astype(BF16)
 
-    for one in AFTER:
-        event(*one)
-
-    def product(d):
-        weight = wbuf[d // N, d % N].reshape(N * WROWS, HEADS * HD)
+
+    def product(p, d):
+        weight = wbuf[d // N, d % N, :, p * PIECE : (p + 1) * PIECE, :].reshape(COLS, HEADS * HD)
         return lax.dot_general(
             abuf[...], weight, (((1,), (1,)), ((), ())), preferred_element_type=F32
         )
 
     def sub(i):
-        first = (1 - c) if i < HALF else c
-        return pl.ds(pl.multiple_of(first * ROWS + (i % HALF) * SUBROWS, SUBROWS), SUBROWS)
-
-    def hop(d, i, send, recv, s_sem, r_sem, to):
+        first = (1 - c) if i == 0 else c
+        return pl.ds(pl.multiple_of(first * ROWS, ROWS), ROWS)
+
+    def hop(p, d, i, send, recv, s_sem, r_sem, to):
         rows = sub(i)
         return pltpu.make_async_remote_copy(
-            src_ref=send.at[d, rows], dst_ref=recv.at[d, rows],
-            send_sem=s_sem.at[d, i], recv_sem=r_sem.at[d, i],
+            src_ref=send.at[p, d, rows], dst_ref=recv.at[p, d, rows],
+            send_sem=s_sem.at[p, d, i], recv_sem=r_sem.at[p, d, i],
             device_id=(me, to), device_id_type=pl.DeviceIdType.MESH,
         )
 
-    def up(d, i):
-        return hop(d, i, up_send, up_recv, usem_s, usem_r, jnp.minimum(tp + 1, TP - 1))
-
-    def down(d, i):
-        return hop(d, i, dn_send, dn_recv, dsem_s, dsem_r, jnp.maximum(tp - 1, 0))
-
-    @pl.loop(0, TP - 1)
-    def _(u):
-        above = TP - 1 - u + tp
-        below = u - TP + 1 + tp
-
-        @pl.when(u >= tp)
-        def _():
-            prod[above] = product(above)
-
-        @pl.when(below >= 0)
-        def _():
-            prod[below] = product(below)
+    def up(p, d, i):
+        return hop(p, d, i, up_send, up_recv, usem_s, usem_r, jnp.minimum(tp + 1, TP - 1))
+
+    def down(p, d, i):
+        return hop(p, d, i, dn_send, dn_recv, dsem_s, dsem_r, jnp.maximum(tp - 1, 0))
+
+    def chain(p, step):
+        nth_up = step - tp
+        nth_down = step - (TP - 1) + tp
+        above = TP - 1 - nth_up
+        above = jnp.where(zh == 0, jnp.where(nth_up < N - 1, above - N, above + N - 1), above)
+        below = nth_down
+        rises = (nth_up >= 0) & (nth_up < TP - 1) & (above > tp)
+        falls = (nth_down >= 0) & (nth_down < TP - 1) & (below < tp)
+        above = jnp.clip(above, 0, TP - 1)
+        below = jnp.clip(below, 0, TP - 1)
+
+        @pl.when(rises)
+        def _():
+            prod[p, above] = product(p, above)
+
+        @pl.when(falls)
+        def _():
+            prod[p, below] = product(p, below)
 
         for i in range(SUB):
             rows = sub(i)
 
-            @pl.when(u >= tp)
+            @pl.when(rises)
             def _():
                 @pl.when(tp > 0)
                 def _():
-                    up(above, i).wait_recv()
-                    up_send[above, rows] = (prod[above, rows] + up_recv[above, rows].astype(F32)).astype(BF16)
+                    up(p, above, i).wait_recv()
+                    up_send[p, above, rows] = (prod[p, above, rows] + up_recv[p, above, rows].astype(F32)).astype(BF16)
 
                 @pl.when(tp == 0)
                 def _():
-                    up_send[above, rows] = prod[above, rows].astype(BF16)
-
-                up(above, i).start()
-
-            @pl.when(below >= 0)
+                    up_send[p, above, rows] = prod[p, above, rows].astype(BF16)
+
+                up(p, above, i).start()
+
+            @pl.when(falls)
             def _():
                 @pl.when(tp < TP - 1)
                 def _():
-                    down(below, i).wait_recv()
-                    dn_send[below, rows] = (prod[below, rows] + dn_recv[below, rows].astype(F32)).astype(BF16)
+                    down(p, below, i).wait_recv()
+                    dn_send[p, below, rows] = (prod[p, below, rows] + dn_recv[p, below, rows].astype(F32)).astype(BF16)
 
                 @pl.when(tp == TP - 1)
                 def _():
-                    dn_send[below, rows] = prod[below, rows].astype(BF16)
-
-                down(below, i).start()
-
-    prod[tp] = product(tp)
-
-    def last(i):
-        rows = pl.ds((i % HALF) * SUBROWS, SUBROWS)
-        return remote(fsend.at[rows], frecv.at[c, rows], SIB_F + i, sib)
-
-    for i in range(SUB):
-        rows = sub(i)
-
-        @pl.when(tp > 0)
-        def _():
-            up(tp, i).wait_recv()
-            prod[tp, rows] += up_recv[tp, rows].astype(F32)
-
-        @pl.when(tp < TP - 1)
-        def _():
-            down(tp, i).wait_recv()
-            prod[tp, rows] += dn_recv[tp, rows].astype(F32)
-
-        part = pl.ds((i % HALF) * SUBROWS, SUBROWS)
-        if i < HALF:
-            fsend[part] = prod[tp, rows].astype(BF16)
-            last(i).start()
-        else:
-            frecv[c, part] = prod[tp, rows].astype(BF16)
-    for i in range(HALF):
-        got(frecv.at[1 - c, pl.ds(i * SUBROWS, SUBROWS)], SIB_F + i)
+                    dn_send[p, below, rows] = prod[p, below, rows].astype(BF16)
+
+                down(p, below, i).start()
+
+    for one in AFTER:
+        event(*one)
+
+    @pl.loop(0, TP + 2)
+    def _(step):
+        for k, events in DURING.items():
+
+            @pl.when((step == k) & (zh == 0))
+            def _():
+                for one in events:
+                    event(*one)
+
+        @pl.when(step == jnp.where(zh == 0, N - 1, jnp.minimum(TP - 1 - tp, tp + N)))
+        def _():
+            for one in LAST:
+                event(*one)
+
+        for p in range(PARTS):
+            chain(p, step)
+
+    for p in range(PARTS):
+        prod[p, tp] = product(p, tp)
+    for inst in (KV, WA, WB, OA, OB):
+        drain(inst)
+
+    def last(p):
+        return remote(fsend.at[p], frecv.at[c, p], SIB_F + p, sib)
+
+    for p in range(PARTS):
+        for i in range(SUB):
+            rows = sub(i)
+
+            @pl.when(tp > 0)
+            def _():
+                up(p, tp, i).wait_recv()
+                prod[p, tp, rows] += up_recv[p, tp, rows].astype(F32)
+
+            @pl.when(tp < TP - 1)
+            def _():
+                down(p, tp, i).wait_recv()
+                prod[p, tp, rows] += dn_recv[p, tp, rows].astype(F32)
+
+            if i == 0:
+                fsend[p] = prod[p, tp, rows].astype(BF16)
+                last(p).start()
+            else:
+                frecv[c, p] = prod[p, tp, rows].astype(BF16)
+    for p in range(PARTS):
+        got(frecv.at[1 - c, p], SIB_F + p)
     for j in range(N):
-        cols = slice(j * WROWS, (j + 1) * WROWS)
+        cols = slice(j * PIECE, (j + 1) * PIECE)
         out[:, j * 2 * WROWS : (j + 1) * 2 * WROWS] = jnp.concatenate(
-            [frecv[0, :, cols], frecv[1, :, cols]], axis=1
+            [frecv[k, p, :, cols] for k in range(2) for p in range(PARTS)], axis=1
         )
 
-    for i in range(HALF):
-        last(i).wait_send()
+    for p in range(PARTS):
+        last(p).wait_send()
     lsend.wait_send()
     for h in range(HEADS):
         oremote(h).wait_send()
-    for inst in (KV, WA, WB, OA, OB):
-        drain(inst)
-
     @pl.when(zh == 1)
     def _():
         drain(KVO)
@@ -408,18 +448,20 @@
 
         @pl.when(tp < d)
         def _():
-            for i in range(SUB):
-                up(d, i).wait_send()
+            for p in range(PARTS):
+                for i in range(SUB):
+                    up(p, d, i).wait_send()
 
         @pl.when(tp > k)
         def _():
-            for i in range(SUB):
-                down(k, i).wait_send()
+            for p in range(PARTS):
+                for i in range(SUB):
+                    down(p, k, i).wait_send()
 
 
 def body(queries, keys, values, out_weight):
     slab = (2, N, N)
-    sums = (TP, BOTH, BOTH)
+    sums = (PARTS, TP, BOTH, COLS)
     return pl.pallas_call(
         kernel,
         out_shape=jax.ShapeDtypeStruct((ROWS, TP * WROWS), BF16),
@@ -443,14 +485,14 @@
             pltpu.VMEM(sums, BF16),
             pltpu.VMEM(sums, BF16),
             pltpu.VMEM(sums, F32),
-            pltpu.VMEM((ROWS, BOTH), BF16),
-            pltpu.VMEM((2, ROWS, BOTH), BF16),
-            pltpu.SemaphoreType.DMA((SIB_F + HALF,)),
-            pltpu.SemaphoreType.DMA((SIB_F + HALF,)),
-            pltpu.SemaphoreType.DMA((TP, SUB)),
-            pltpu.SemaphoreType.DMA((TP, SUB)),
-            pltpu.SemaphoreType.DMA((TP, SUB)),
-            pltpu.SemaphoreType.DMA((TP, SUB)),
+            pltpu.VMEM((PARTS, ROWS, COLS), BF16),
+            pltpu.VMEM((2, PARTS, ROWS, COLS), BF16),
+            pltpu.SemaphoreType.DMA((SIB_F + PARTS,)),
+            pltpu.SemaphoreType.DMA((SIB_F + PARTS,)),
+            pltpu.SemaphoreType.DMA((PARTS, TP, SUB)),
+            pltpu.SemaphoreType.DMA((PARTS, TP, SUB)),
+            pltpu.SemaphoreType.DMA((PARTS, TP, SUB)),
+            pltpu.SemaphoreType.DMA((PARTS, TP, SUB)),
             pltpu.SemaphoreType.DMA((4,)),
         ],
         compiler_params=pltpu.CompilerParams(

time: 84.6 us -> 82.3 us (0.973)
  the two profiles are of different devices: /device:TPU:1 before, /device:TPU:385 now
where the time goes in v4:
time: 82.3 us; the launch traced here: 82.1 us
  Pallas kernels  80.6 us (98%)
  local copies, waits for them, and re-layouts  1.57 us (2%)
    pallas_call x1, Pallas kernels, body(): pl.pallas_call(kernel, out_shape=jax.ShapeDtypeStruct((ROWS, TP * WROWS),...  80.6 us

profile of v4, /device:TPU:385, one launch (start us, length us, event | category | flops | bytes accessed | tf_op | source)
XLA Modules:
  0.0 82.1 jit_solution(17913399561011667332)
XLA Ops:
  0.0 80.6 %shard_map.46 = bf16[128,512]{1,0:T(8,128)(2,1)} custom-call(bf16[128,1024]{1,0:T(8,128)(2,1)} %q_in.1, bf16[128,128]{1,0:T(8,128)(2,1)} %k_in.1, bf16[128,128]{1,0:T(8,128)(2,1)} %v_in.1, bf16[64,1024]{1,0:T(8,128)(2,1)} %w_in.1), custom_call_target="tpu_custom_call" | custom-call | flops 5000000000 | bytes 1048576 | tf_op jit(solution)/shard_map/pallas_call | solution.py:465
  80.6 1.6 %copy.6 = bf16[128,512]{1,0:T(8,128)(2,1)} copy(bf16[128,512]{1,0:T(8,128)(2,1)} %shard_map.46) | data formatting | bytes 262144

commit v5 on v4

--- a/solution.py
+++ b/solution.py
@@ -34,7 +34,7 @@
 LAST_HALF_MORE = {0:[(OB,1)],3:[(OA,2)],5:[(OB,2)]}
 AFTER = [(WA, 3), (WB, 3)]
 DURING = {1: [(OA, 2)], 2: [(OB, 2)]}
-LAST = [(OA, 3), (OB, 3)]
+LAST = [(OA, 3)], [(OB, 3)]
 CROSS_K, CROSS_V, CROSS_W, SIB_Q, SIB_L, SIB_O, SIB_F = 96, 97, 98, 100, 101, 102, 110
 
 
@@ -381,18 +381,36 @@
                 for one in events:
                     event(*one)
 
-        @pl.when(step == jnp.where(zh == 0, N - 1, jnp.minimum(TP - 1 - tp, tp + N)))
-        def _():
-            for one in LAST:
-                event(*one)
-
+        first = jnp.where(zh == 0, N - 1, jnp.minimum(TP - 1 - tp, tp + N))
         for p in range(PARTS):
+
+            @pl.when(step == first)
+            def _():
+                for one in LAST[p]:
+                    event(*one)
+
             chain(p, step)
 
     for p in range(PARTS):
         prod[p, tp] = product(p, tp)
     for inst in (KV, WA, WB, OA, OB):
         drain(inst)
+    lsend.wait_send()
+    for h in range(HEADS):
+        oremote(h).wait_send()
+    @pl.when(zh == 1)
+    def _():
+        drain(KVO)
+
+    @pl.when(zh == 0)
+    def _():
+        remote(kbuf.at[zh, x, y], kbuf.at[zh, x, y], CROSS_K, zz).wait_send()
+        remote(vbuf.at[zh, x, y], vbuf.at[zh, x, y], CROSS_V, zz).wait_send()
+
+    cross(0).wait_send()
+    cross(1).wait_send()
+    remote(qbuf.at[c], qbuf.at[c], SIB_Q, sib).wait_send()
+
 
     def last(p):
         return remote(fsend.at[p], frecv.at[c, p], SIB_F + p, sib)
@@ -426,22 +444,6 @@
 
     for p in range(PARTS):
         last(p).wait_send()
-    lsend.wait_send()
-    for h in range(HEADS):
-        oremote(h).wait_send()
-    @pl.when(zh == 1)
-    def _():
-        drain(KVO)
-
-    @pl.when(zh == 0)
-    def _():
-        remote(kbuf.at[zh, x, y], kbuf.at[zh, x, y], CROSS_K, zz).wait_send()
-        remote(vbuf.at[zh, x, y], vbuf.at[zh, x, y], CROSS_V, zz).wait_send()
-
-    cross(0).wait_send()
-    cross(1).wait_send()
-    remote(qbuf.at[c], qbuf.at[c], SIB_Q, sib).wait_send()
-
     @pl.loop(0, TP - 1)
     def _(k):
         d = TP - 1 - k

time: 82.3 us -> 82.2 us (level)
  no operation moved by 1% of the time
where the time goes in v5:
time: 82.2 us; the launch traced here: 82.1 us
  Pallas kernels  80.5 us (98%)
  local copies, waits for them, and re-layouts  1.57 us (2%)
    pallas_call x1, Pallas kernels, body(): pl.pallas_call(kernel, out_shape=jax.ShapeDtypeStruct((ROWS, TP * WROWS),...  80.5 us

profile of v5, /device:TPU:385, one launch (start us, length us, event | category | flops | bytes accessed | tf_op | source)
XLA Modules:
  0.0 82.1 jit_solution(12362780943647983722)
XLA Ops:
  0.0 80.5 %shard_map.46 = bf16[128,512]{1,0:T(8,128)(2,1)} custom-call(bf16[128,1024]{1,0:T(8,128)(2,1)} %q_in.1, bf16[128,128]{1,0:T(8,128)(2,1)} %k_in.1, bf16[128,128]{1,0:T(8,128)(2,1)} %v_in.1, bf16[64,1024]{1,0:T(8,128)(2,1)} %w_in.1), custom_call_target="tpu_custom_call" | custom-call | flops 5000000000 | bytes 1048576 | tf_op jit(solution)/shard_map/pallas_call | solution.py:467
  80.5 1.6 %copy.6 = bf16[128,512]{1,0:T(8,128)(2,1)} copy(bf16[128,512]{1,0:T(8,128)(2,1)} %shard_map.46) | data formatting | bytes 262144
